TPU v7x, 32 devices: a whole 2x2x4 slice. The times are simulated.
32 devices in a mesh: group: 2 (over y), dm: 4 (over z), tm: 2 (over x), beam: 2 (over core).
Axes of the slice: x: 2, y: 2, z: 4, core: 2. Of those that a mesh axis runs over, the one named last changes fastest.
Arguments:
- raw: bfloat16 [16, 4194304], P(('group', 'dm', 'beam'), 'tm'), parts along dimension 0
- proto: float32 [4, 16384], replicated, may hold values from -4 to 4
- delays: int32 [8, 4, 64], replicated, may hold values from 0 to 3, as said below
- widths: int32 [8], replicated, may hold values from 1 to 8, as said below
- owners: int32 [8, 1], replicated, may hold values from 0 to 3; in each aligned block of 8 rows (0 to 7, 8 to 15, ...) at most 4 rows name the same one
Outputs:
- detect: bfloat16 [16, 8, 2, 4, 8, 256], P('dm', 'group', 'beam', None, None, 'tm'), parts along dimension 1
There are 2 independent parts, one for each index of `group`. A program takes and returns all parts, laid end to end along the dimension named above; an argument that names none is the same for every part. Nothing has to cross between parts.
Inputs may be any that keep to these rules, and one draw needn't show every extreme that they name: `delays`: 3 occurs in every draw. `widths`: 8 occurs in every draw. `owners`: each owner holds at most 4 DM blocks, and some owner holds exactly 4.
All inputs are finite; a program needn't handle non-finite values.
Results may differ from a plain program's by a relative error of at most 0.014.
Values may be sent and summed in bfloat16 or wider, within the bound.
A program may use at most 128 MiB of HBM per device.

v0:
```python
import math

import jax
import jax.numpy as jnp
from jax import lax
from jax.sharding import PartitionSpec as P

DFT_A = 128
NBLK = 64
PFB_BLK = 16
FD = 4
TT = 8
MAXT = 3
WMAX = 8


def shifted(value, axis, steps):
    count = lax.axis_size(axis)
    first, last = (max(0, -steps), min(count, count - steps))
    return lax.ppermute(value, axis, [(source, source + steps) for source in range(first, last)])


def dft_tables(size):
    index = jnp.arange(size, dtype=jnp.int32)
    product = index[:, None] * index[None, :] % size
    angle = product.astype(jnp.float32) * (2.0 * math.pi / size)
    return (jnp.cos(angle).astype(jnp.bfloat16), jnp.sin(angle).astype(jnp.bfloat16))


def twiddle_tables(rows, cols, total):
    first = jnp.arange(rows, dtype=jnp.int32)
    second = jnp.arange(cols, dtype=jnp.int32)
    product = first[:, None] * second[None, :] % total
    angle = product.astype(jnp.float32) * (2.0 * math.pi / total)
    return (jnp.cos(angle), jnp.sin(angle))


def spectra_power(window_frames, proto):
    taps, channels = proto.shape
    beams_here = window_frames.shape[0]
    count = window_frames.shape[1] - taps + 1
    side_b = channels // DFT_A
    acc = window_frames[:, 0:count].astype(jnp.float32) * proto[0]
    for tap in range(1, taps):
        acc = acc + window_frames[:, tap : tap + count].astype(jnp.float32) * proto[tap]
    frames_bf = acc.astype(jnp.bfloat16).reshape(beams_here * count, DFT_A, side_b)
    cos_a, sin_a = dft_tables(DFT_A)
    cos_b, sin_b = dft_tables(side_b)
    tw_cos, tw_sin = twiddle_tables(side_b, DFT_A, channels)
    a_re = jnp.einsum("kab,fa->kbf", frames_bf, cos_a, preferred_element_type=jnp.float32)
    a_im = -jnp.einsum("kab,fa->kbf", frames_bf, sin_a, preferred_element_type=jnp.float32)
    t_re = (a_re * tw_cos + a_im * tw_sin).astype(jnp.bfloat16)
    t_im = (a_im * tw_cos - a_re * tw_sin).astype(jnp.bfloat16)
    c_re = jnp.einsum("kbf,gb->kgf", t_re, cos_b, preferred_element_type=jnp.float32) + jnp.einsum(
        "kbf,gb->kgf", t_im, sin_b, preferred_element_type=jnp.float32
    )
    c_im = jnp.einsum("kbf,gb->kgf", t_im, cos_b, preferred_element_type=jnp.float32) - jnp.einsum(
        "kbf,gb->kgf", t_re, sin_b, preferred_element_type=jnp.float32
    )
    power = (c_re * c_re + c_im * c_im) * (1.0 / (taps * channels))
    return power.reshape(beams_here, count, channels)


def blocked_power(extended, proto, first, count):
    taps = proto.shape[0]

    def block_power(index):
        start = first + index * PFB_BLK
        window = lax.dynamic_slice_in_dim(extended, start, PFB_BLK + taps - 1, 1)
        return spectra_power(window, proto)

    blocks = lax.map(block_power, jnp.arange(count // PFB_BLK, dtype=jnp.int32))
    beams_here = extended.shape[0]
    return jnp.moveaxis(blocks, 0, 1).reshape(beams_here, count, extended.shape[2])


def fine_masks(groups, width):
    block = jnp.arange(groups, dtype=jnp.int32)[:, None]
    inner = jnp.arange(width, dtype=jnp.int32)[None, :]
    fine = block * FD * (width - 1 - inner) // (groups * (width - 1))
    return jnp.stack([(fine == step).astype(jnp.bfloat16) for step in range(FD)])


def subband_sums(flat_ext, groups, count):
    beams_here, length, channels = flat_ext.shape
    width = channels // NBLK
    view = flat_ext.reshape(beams_here, length, NBLK, width)
    masks = fine_masks(groups, width)
    total = jnp.zeros((beams_here, groups, NBLK, count), jnp.float32)
    for step in range(FD):
        part = view[:, FD - 1 - step : FD - 1 - step + count]
        total = total + jnp.einsum(
            "bkci,gi->bgck", part, masks[step], preferred_element_type=jnp.float32
        )
    return (total * (1.0 / math.sqrt(width))).astype(jnp.bfloat16)


def dedisperse(extended, delays, count):
    length = count + WMAX - 1
    total = 0.0
    for value in range(MAXT + 1):
        start = (MAXT - value) * TT
        window = extended[..., start : start + length]
        mask = (delays == value).astype(jnp.bfloat16)
        total = total + jnp.einsum(
            "rgck,gjc->rgjk", window, mask, preferred_element_type=jnp.float32
        )
    return total * (1.0 / math.sqrt(NBLK))


def boxcar(series, widths, count):
    lags = jnp.arange(WMAX, dtype=jnp.int32)
    weights = (lags[None, :] < widths[:, None]).astype(jnp.float32) / jnp.sqrt(
        widths.astype(jnp.float32)
    )[:, None]
    stacked = jnp.stack(
        [series[..., WMAX - 1 - lag : WMAX - 1 - lag + count] for lag in range(WMAX)], -2
    )
    return jnp.einsum("rgjik,wi->rgjwk", stacked, weights)


def slot_table(owners, owner_count, capacity):
    owner = owners[:, 0]
    groups = owner.shape[0]
    index = jnp.arange(groups, dtype=jnp.int32)
    same = owner[:, None] == owner[None, :]
    earlier = index[None, :] < index[:, None]
    rank = jnp.sum((same & earlier).astype(jnp.int32), 1)
    hit_owner = owner[None, None, :] == jnp.arange(owner_count, dtype=jnp.int32)[:, None, None]
    hit_slot = rank[None, None, :] == jnp.arange(capacity, dtype=jnp.int32)[None, :, None]
    return (hit_owner & hit_slot).astype(jnp.int32)


def shards(raw, proto, delays, widths, owners):
    taps, channels = proto.shape
    beams_here = raw.shape[0]
    spec = raw.shape[1] // channels
    groups = delays.shape[0]
    owner_count = lax.axis_size("dm")
    capacity = 2 * (groups // owner_count)
    halo = MAXT * TT + WMAX - 1
    frames = raw.reshape(beams_here, spec, channels)
    total_spectra = spec * lax.axis_size("tm")
    history = taps - 1 + FD - 1
    before = shifted(frames[:, spec - history :], "tm", 1)
    extended = jnp.concatenate([before, frames], 1)
    early_power = spectra_power(extended[:, 0 : FD - 1 + taps - 1], proto)
    main_power = blocked_power(extended, proto, FD - 1, spec)
    band = lax.psum(jnp.sum(main_power, 1), "tm") / total_spectra
    ratio = jnp.concatenate([early_power, main_power], 1) / (band[:, None, :] + 1e-06)
    flat_ext = (ratio - jnp.mean(ratio, 2, keepdims=True)).astype(jnp.bfloat16)
    sub = subband_sums(flat_ext, groups, spec)
    table = slot_table(owners, owner_count, capacity)
    table_bf = table.astype(jnp.bfloat16)
    packed = jnp.einsum(
        "osg,bgck->obsck", table_bf, sub, preferred_element_type=jnp.float32
    ).astype(jnp.bfloat16)
    received = lax.all_to_all(packed, "dm", split_axis=0, concat_axis=1, tiled=True)[0]
    earlier_sub = shifted(received[..., spec - halo :], "tm", 1)
    owned = jnp.concatenate([earlier_sub, received], -1)
    mine = lax.dynamic_index_in_dim(table, lax.axis_index("dm"), 0, keepdims=False)
    slot_delays = jnp.sum(mine[:, :, None, None] * delays[None], 1)
    series = dedisperse(owned, slot_delays, spec)
    box = boxcar(series, widths, spec).astype(jnp.bfloat16)
    result = jnp.transpose(box, (1, 0, 2, 3, 4))
    return result.reshape(capacity, owner_count, beams_here, result.shape[2], result.shape[3], spec)


def solution(mesh):
    return jax.shard_map(
        shards,
        mesh=mesh,
        in_specs=(P(("group", "dm", "beam"), "tm"), P(), P(), P(), P()),
        out_specs=P("dm", "group", "beam", None, None, "tm"),
        check_vma=False,
    )
```

profile of v0, /device:TPU:0, one launch (start us, length us, event | category | flops | bytes accessed | tf_op | source)
XLA Modules:
  0.0 273.6 jit_solution(5279019373399987779)
XLA Ops:
  6.5 90.0 %reduce.3 = bf16[2097152]{0:T(1024)(128)(2,1)} reduce(bf16[1,2097152]{1,0:T(2,128)(2,1)} %param.7, bf16[]{:T(256)} %constant.179), dimensions={0}, to_apply=%param.7.reduce_sub_computation | reduce | bytes 8388610 | tf_op args[0]
  96.5 7.3 %reshape.370 = bf16[1,128,16384]{2,1,0:T(8,128)(2,1)} reshape(bf16[2097152]{0:T(1024)(128)(2,1)} %reduce.3) | data formatting | bytes 8388608 | tf_op jit(solution)/shard_map/reshape | solution.py:142
  103.9 1.0 slice.160
  104.9 5.0 %collective-permute-start = (bf16[1,6,16384]{2,1,0:T(8,128)(2,1)S(1)}, bf16[1,6,16384]{2,1,0:T(8,128)(2,1)S(1)}, u32[]{:S(2)}, u32[]{:S(2)}) collective-permute-start(bf16[1,6,16384]{2,1,0:T(8,128)(2,1)S(1)} %slice.160), channel_id=1, source_target_pairs={{0,2},{1,3},{4,6},{5,7},{8,10},{9,11},{12,14},{13,15},{16,18},{17,... | collective-permute-start | bytes 589832 | tf_op jit(solution)/shard_map/ppermute | solution.py:20
  110.6 4.6 %collective-permute-done = bf16[1,6,16384]{2,1,0:T(8,128)(2,1)S(1)} collective-permute-done((bf16[1,6,16384]{2,1,0:T(8,128)(2,1)S(1)}, bf16[1,6,16384]{2,1,0:T(8,128)(2,1)S(1)}, u32[]{:S(2)}, u32[]{:S(2)}) %collective-permute-start) | collective-permute-done | bytes 196640 | tf_op jit(solution)/shard_map/ppermute | solution.py:20
  117.6 5.4 %pad_maximum_fusion = bf16[1,134,16384]{2,1,0:T(8,128)(2,1)} fusion(bf16[1,128,16384]{2,1,0:T(8,128)(2,1)} %reshape.370, bf16[1,6,16384]{2,1,0:T(8,128)(2,1)S(1)} %collective-permute-done), kind=kLoop, calls=%fused_computation.68 | loop fusion | flops 8781824 | bytes 8781824 | tf_op jit(solution)/shard_map/concatenate | solution.py:146
  122.9 75.4 %while.13 = (s32[]{:T(128)}, f32[8,1,16,16384]{3,2,1,0:T(8,128)}, s32[8]{0:T(128)S(1)}, bf16[1,134,16384]{2,1,0:T(8,128)(2,1)}, f32[4,16384]{1,0:T(4,128)S(1)}, ...) while((s32[]{:T(128)}, f32[8,1,16,16384]{3,2,1,0:T(8,128)}, ...), condition=%wide.region_3.4_spmd, body=%wide.region_2.3_spmd.sunk | while | flops 411435008 | bytes 22545144 | solution.py:72
  124.4 3.3 %fusion.264 = bf16[2,8,128,128]{3,1,2,0:T(8,128)(2,1)S(1)} fusion(bf16[1,134,16384]{2,1,0:T(8,128)(2,1)} %get-tuple-element.202, s32[]{:T(128)S(6)} %add.420, s32[]{:T(128)S(6)} %add.421, s32[]{:T(128)S(6)} %add.422, s32[]{:T(128)S(6)} %select_n.191, f32[16384]{0:T(1024)S(1)} %bitcast.245, f32[16384]{0:T(1024)S(1)} %bitcast.246, ...), kind=kLoop, calls=%fused_computation.11.clone.1 | loop fusion | flops 3145728 | bytes 2883600 | tf_op jit(solution)/shard_map/while
  128.6 0.7 subtract_convert_fusion.3
  131.5 1.1 constant_dynamic-update-slice_fusion.2
  134.1 3.2 %fusion.264 = bf16[2,8,128,128]{3,1,2,0:T(8,128)(2,1)S(1)} fusion(bf16[1,134,16384]{2,1,0:T(8,128)(2,1)} %get-tuple-element.202, s32[]{:T(128)S(6)} %add.420, s32[]{:T(128)S(6)} %add.421, s32[]{:T(128)S(6)} %add.422, s32[]{:T(128)S(6)} %select_n.191, f32[16384]{0:T(1024)S(1)} %bitcast.245, f32[16384]{0:T(1024)S(1)} %bitcast.246, ...), kind=kLoop, calls=%fused_computation.11.clone.1 | loop fusion | flops 3145728 | bytes 2883600 | tf_op jit(solution)/shard_map/while
  138.2 0.7 subtract_convert_fusion.3
  141.1 1.1 constant_dynamic-update-slice_fusion.2
  143.7 3.0 %fusion.264 = bf16[2,8,128,128]{3,1,2,0:T(8,128)(2,1)S(1)} fusion(bf16[1,134,16384]{2,1,0:T(8,128)(2,1)} %get-tuple-element.202, s32[]{:T(128)S(6)} %add.420, s32[]{:T(128)S(6)} %add.421, s32[]{:T(128)S(6)} %add.422, s32[]{:T(128)S(6)} %select_n.191, f32[16384]{0:T(1024)S(1)} %bitcast.245, f32[16384]{0:T(1024)S(1)} %bitcast.246, ...), kind=kLoop, calls=%fused_computation.11.clone.1 | loop fusion | flops 3145728 | bytes 2883600 | tf_op jit(solution)/shard_map/while
  147.6 0.7 subtract_convert_fusion.3
  150.5 1.1 constant_dynamic-update-slice_fusion.2
  153.1 3.0 %fusion.264 = bf16[2,8,128,128]{3,1,2,0:T(8,128)(2,1)S(1)} fusion(bf16[1,134,16384]{2,1,0:T(8,128)(2,1)} %get-tuple-element.202, s32[]{:T(128)S(6)} %add.420, s32[]{:T(128)S(6)} %add.421, s32[]{:T(128)S(6)} %add.422, s32[]{:T(128)S(6)} %select_n.191, f32[16384]{0:T(1024)S(1)} %bitcast.245, f32[16384]{0:T(1024)S(1)} %bitcast.246, ...), kind=kLoop, calls=%fused_computation.11.clone.1 | loop fusion | flops 3145728 | bytes 2883600 | tf_op jit(solution)/shard_map/while
  157.0 0.7 subtract_convert_fusion.3
  159.9 1.1 constant_dynamic-update-slice_fusion.2
  162.5 2.9 %fusion.264 = bf16[2,8,128,128]{3,1,2,0:T(8,128)(2,1)S(1)} fusion(bf16[1,134,16384]{2,1,0:T(8,128)(2,1)} %get-tuple-element.202, s32[]{:T(128)S(6)} %add.420, s32[]{:T(128)S(6)} %add.421, s32[]{:T(128)S(6)} %add.422, s32[]{:T(128)S(6)} %select_n.191, f32[16384]{0:T(1024)S(1)} %bitcast.245, f32[16384]{0:T(1024)S(1)} %bitcast.246, ...), kind=kLoop, calls=%fused_computation.11.clone.1 | loop fusion | flops 3145728 | bytes 2883600 | tf_op jit(solution)/shard_map/while
  166.3 0.7 subtract_convert_fusion.3
  169.2 1.0 constant_dynamic-update-slice_fusion.2
  171.8 3.0 %fusion.264 = bf16[2,8,128,128]{3,1,2,0:T(8,128)(2,1)S(1)} fusion(bf16[1,134,16384]{2,1,0:T(8,128)(2,1)} %get-tuple-element.202, s32[]{:T(128)S(6)} %add.420, s32[]{:T(128)S(6)} %add.421, s32[]{:T(128)S(6)} %add.422, s32[]{:T(128)S(6)} %select_n.191, f32[16384]{0:T(1024)S(1)} %bitcast.245, f32[16384]{0:T(1024)S(1)} %bitcast.246, ...), kind=kLoop, calls=%fused_computation.11.clone.1 | loop fusion | flops 3145728 | bytes 2883600 | tf_op jit(solution)/shard_map/while
  175.7 0.7 subtract_convert_fusion.3
  178.6 1.1 constant_dynamic-update-slice_fusion.2
  181.2 2.9 %fusion.264 = bf16[2,8,128,128]{3,1,2,0:T(8,128)(2,1)S(1)} fusion(bf16[1,134,16384]{2,1,0:T(8,128)(2,1)} %get-tuple-element.202, s32[]{:T(128)S(6)} %add.420, s32[]{:T(128)S(6)} %add.421, s32[]{:T(128)S(6)} %add.422, s32[]{:T(128)S(6)} %select_n.191, f32[16384]{0:T(1024)S(1)} %bitcast.245, f32[16384]{0:T(1024)S(1)} %bitcast.246, ...), kind=kLoop, calls=%fused_computation.11.clone.1 | loop fusion | flops 3145728 | bytes 2883600 | tf_op jit(solution)/shard_map/while
  185.0 0.7 subtract_convert_fusion.3
  188.0 1.1 constant_dynamic-update-slice_fusion.2
  190.5 2.9 %fusion.264 = bf16[2,8,128,128]{3,1,2,0:T(8,128)(2,1)S(1)} fusion(bf16[1,134,16384]{2,1,0:T(8,128)(2,1)} %get-tuple-element.202, s32[]{:T(128)S(6)} %add.420, s32[]{:T(128)S(6)} %add.421, s32[]{:T(128)S(6)} %add.422, s32[]{:T(128)S(6)} %select_n.191, f32[16384]{0:T(1024)S(1)} %bitcast.245, f32[16384]{0:T(1024)S(1)} %bitcast.246, ...), kind=kLoop, calls=%fused_computation.11.clone.1 | loop fusion | flops 3145728 | bytes 2883600 | tf_op jit(solution)/shard_map/while
  194.3 0.7 subtract_convert_fusion.3
  197.2 1.1 constant_dynamic-update-slice_fusion.2
  198.3 4.5 %reduce_sum.40 = f32[16384]{0:T(1024)} reduce(f32[8,1,16,16384]{3,2,1,0:T(8,128)} %get-tuple-element.95, f32[]{:T(128)} %constant.170.clone.1), dimensions={0,1,2}, to_apply=%region_4.5 | reduce | flops 2080768 | bytes 8454148 | tf_op jit(solution)/shard_map/reduce_sum | solution.py:149
  203.5 6.0 %copy.62 = f32[16,8,64,256]{3,2,1,0:T(8,128)S(1)} copy(f32[16,8,64,256]{3,1,2,0:T(8,128)} %bitcast.241) | data formatting | bytes 16777216
  209.5 8.1 %copy.45 = f32[1,128,64,256]{3,1,2,0:T(8,128)} copy(f32[1,128,64,256]{3,2,1,0:T(8,128)S(1)} %bitcast.243) | data formatting | bytes 16777216 | tf_op jit(solution)/shard_map/concatenate | solution.py:150
  217.6 8.4 %all-reduce.2.cloned.1.call-done = f32[1,16384]{1,0:T(1,128)} async-done(((f32[1,16384]{1,0:T(1,128)}), f32[1,16384]{1,0:T(1,128)}) %all-reduce.2.cloned.1.call-update) | async-done | bytes 65552 | tf_op jit(solution)/shard_map/psum | solution.py:149
  226.0 1.1 fusion.221
  227.0 4.2 %fusion.56 = f32[131]{0:T(256)S(1)} fusion(f32[1,128,16384]{2,1,0:T(8,128)} %bitcast.242, f32[1,3,16384]{2,1,0:T(4,128)S(1)} %concatenate.39, f32[16384]{0:T(1024)S(1)} %bitcast.253), kind=kLoop, calls=%fused_computation.67 | loop fusion | flops 6438781 | bytes 8651276 | tf_op jit(solution)/shard_map/reduce_sum | solution.py:151
  231.3 4.8 %fusion.55 = bf16[1,131,64,256]{3,1,2,0:T(8,128)(2,1)S(1)} fusion(f32[1,128,64,256]{3,1,2,0:T(8,128)} %copy.45, f32[1,3,64,256]{3,1,2,0:T(4,128)S(1)} %copy.44, f32[131]{0:T(256)S(1)} %broadcast_multiply_fusion, f32[64,256]{1,0:T(8,128)S(1)} %add.239), kind=kLoop, calls=%fused_computation.65 | loop fusion | flops 8585216 | bytes 12943884 | tf_op jit(solution)/shard_map/convert_element_type | solution.py:151
  236.1 1.2 fusion.59
  237.3 1.2 fusion.65
  238.5 1.2 fusion.64
  239.7 3.6 %fusion.61 = bf16[4,1,4,64,128]{4,2,0,3,1:T(4,128)(2,1)S(1)} fusion(f32[8,128,64]{1,0,2:T(8,128)S(1)} %fusion.64, bf16[1,131,64,256]{3,1,2,0:T(8,128)(2,1)} %copy-done, s32[256]{0:T(256)S(1)} %iota_subtract_fusion, s32[8]{0:T(128)S(1)} %iota_multiply_fusion.2, pred[4,8]{1,0:T(4,128)(4,1)S(1)} %get-tuple-element.124, pred[4,8]{1,0:T(4,128)(4,1)S(1)} %get-tuple-element.125), kind=kOutput, calls=%fused_computation.78 | convolution fusion | flops 36000128 | bytes 4719712 | tf_op jit(solution)/shard_map/osg,bgck->obsck/dot_general | solution.py:155
  243.3 0.8 copy.46
  244.1 4.6 %all-to-all-start = ((bf16[4,1,4,64,128]{4,2,3,1,0:T(4,128)(2,1)}), bf16[4,1,4,64,128]{4,2,3,1,0:T(4,128)(2,1)S(1)}, u32[]{:S(2)}, u32[]{:S(2)}) async-start(bf16[4,1,4,64,128]{4,2,3,1,0:T(4,128)(2,1)} %copy.46), calls=%async_computation | async-start | bytes 524288 | tf_op jit(solution)/shard_map/all_to_all | solution.py:158
  248.8 8.4 %all-to-all-done = bf16[4,1,4,64,128]{4,2,3,1,0:T(4,128)(2,1)S(1)} async-done(((bf16[4,1,4,64,128]{4,2,3,1,0:T(4,128)(2,1)}), bf16[4,1,4,64,128]{4,2,3,1,0:T(4,128)(2,1)S(1)}, u32[]{:S(2)}, u32[]{:S(2)}) %all-to-all-start) | async-done | bytes 262176 | tf_op jit(solution)/shard_map/all_to_all | solution.py:158
  257.4 2.5 collective-permute-start.1
  259.9 3.8 %collective-permute-done.1 = bf16[4,4,64,31]{3,2,0,1:T(8,128)(2,1)S(1)} collective-permute-done((bf16[4,4,64,31]{3,2,0,1:T(8,128)(2,1)S(1)}, bf16[4,4,64,31]{3,2,0,1:T(8,128)(2,1)S(1)}, u32[]{:S(2)}, u32[]{:S(2)}) %collective-permute-start.1) | collective-permute-done | bytes 63520 | tf_op jit(solution)/shard_map/ppermute | solution.py:20
  266.1 0.7 copy.49
  (132 shorter events, 37.9 us)
Async XLA Ops:
  6.5 103.7 %copy-start.1 = (f32[4,16384]{1,0:T(4,128)S(1)}, f32[4,16384]{1,0:T(4,128)}, u32[]{:S(2)}) copy-start(f32[4,16384]{1,0:T(4,128)} %param.8) | copy-start | bytes 786436
  6.5 103.9 %copy-start.4 = (s32[8,1]{0,1:T(1,128)S(1)}, s32[8,1]{0,1:T(1,128)}, u32[]{:S(2)}) copy-start(s32[8,1]{0,1:T(1,128)} %param.11) | copy-start | bytes 100
  6.5 219.4 %all-reduce.2.cloned.1.call-start = ((), (), s32[]{:S(2)}) async-start(), calls=%async_computation.1 | async-start | bytes 131072 | tf_op jit(solution)/shard_map/psum | solution.py:149
  104.9 10.4 %collective-permute-start = (bf16[1,6,16384]{2,1,0:T(8,128)(2,1)S(1)}, bf16[1,6,16384]{2,1,0:T(8,128)(2,1)S(1)}, u32[]{:S(2)}, u32[]{:S(2)}) collective-permute-start(bf16[1,6,16384]{2,1,0:T(8,128)(2,1)S(1)} %slice.160), channel_id=1, source_target_pairs={{0,2},{1,3},{4,6},{5,7},{8,10},{9,11},{12,14},{13,15},{16,18},{17,... | collective-permute-start | bytes 589832 | tf_op jit(solution)/shard_map/ppermute | solution.py:20
  236.1 2.4 copy-start
  238.5 10.2 %copy-start.2 = (s32[8,4,64]{2,1,0:T(4,128)S(1)}, s32[8,4,64]{2,1,0:T(4,128)}, u32[]{:S(2)}) copy-start(s32[8,4,64]{2,1,0:T(4,128)} %param.9) | copy-start | bytes 24580
  238.5 10.2 %copy-start.3 = (s32[8]{0:T(128)S(1)}, s32[8]{0:T(128)}, u32[]{:S(2)}) copy-start(s32[8]{0:T(128)} %param.10) | copy-start | bytes 100
  244.1 13.0 %all-to-all-start = ((bf16[4,1,4,64,128]{4,2,3,1,0:T(4,128)(2,1)}), bf16[4,1,4,64,128]{4,2,3,1,0:T(4,128)(2,1)S(1)}, u32[]{:S(2)}, u32[]{:S(2)}) async-start(bf16[4,1,4,64,128]{4,2,3,1,0:T(4,128)(2,1)} %copy.46), calls=%async_computation | async-start | bytes 524288 | tf_op jit(solution)/shard_map/all_to_all | solution.py:158
  257.4 6.3 %collective-permute-start.1 = (bf16[4,4,64,31]{3,2,0,1:T(8,128)(2,1)S(1)}, bf16[4,4,64,31]{3,2,0,1:T(8,128)(2,1)S(1)}, u32[]{:S(2)}, u32[]{:S(2)}) collective-permute-start(bf16[4,4,64,31]{3,2,0,1:T(8,128)(2,1)S(1)} %slice.169), channel_id=1, source_target_pairs={{0,2},{1,3},{4,6},{5,7},{8,10},{9,11},{12,14},{13,15},{16,18},{17,... | collective-permute-start | bytes 190472 | tf_op jit(solution)/shard_map/ppermute | solution.py:20
Sparse Core Ops, SparseCore 0:
  202.9 22.9 all-reduce.1
where the time goes:
time: 274 us
  other arithmetic  137 us (50%)
  local copies, waits for them, and re-layouts  42.6 us (16%)
  matrix products  37.3 us (14%)
  waiting for transfers between devices  25.2 us (9%)
  between operations  13.6 us (5%)
  starting transfers between devices  12.1 us (4%)
  loops' own time  5.67 us (2%)
    unnamed x2, other arithmetic  90.3 us
    while x8, other arithmetic  24.1 us
    dynamic_update_slice x8, local copies, waits for them, and re-layouts, blocked_power(): blocks = lax.map(block_power, jnp.arange(count // PFB_BLK, dtype=jnp.int32))  8.56 us
    psum x1, waiting for transfers between devices, shards(): band = lax.psum(jnp.sum(main_power, 1), 'tm') / total_spectra  8.4 us
    ppermute x2, waiting for transfers between devices, shifted(): lax.ppermute(value, axis, [(source, source + steps) for source in range(f...  8.39 us
    all_to_all x1, waiting for transfers between devices, shards(): lax.all_to_all(packed, 'dm', split_axis=0, concat_axis=1, tiled=True)[0]  8.38 us
    concatenate x4, local copies, waits for them, and re-layouts, shards(): jnp.concatenate([early_power, main_power], 1) / (band[:, None, :] + 1e-06)  8.35 us
    ppermute x2, starting transfers between devices, shifted(): lax.ppermute(value, axis, [(source, source + steps) for source in range(f...  7.52 us
  transfers between devices with their start and end apart: 4, of which 4 were waited for; matrix products, arithmetic and copies ran while one was open for 6% of the time, Pallas kernels for 0%

commit v1 on v0

v1 whole, which is shorter than its diff:
```python
import functools
import math

import jax
import jax.numpy as jnp
import numpy as np
from jax import lax
from jax.experimental import pallas as pl
from jax.experimental.pallas import tpu as pltpu
from jax.sharding import PartitionSpec as P

SIDE = 128
NBLK = 64
FD = 4
TT = 8
MAXT = 3
WMAX = 8
SPB = 8
F32 = jnp.float32
BF16 = jnp.bfloat16


def shifted(value, axis, steps):
    count = lax.axis_size(axis)
    return lax.ppermute(value, axis, [(s, s + steps) for s in range(count - steps)])


def tables(channels):
    i = np.arange(SIDE)
    ang = (i[:, None] * i[None, :] % SIDE) * (2.0 * math.pi / SIDE)
    c, s = np.cos(ang), np.sin(ang)
    w1 = np.concatenate([c, s], 0)
    w2 = np.block([[c, -s], [-s, -c]])
    tw = (i[:, None] * i[None, :] % channels) * (2.0 * math.pi / channels)
    twiddle = np.stack([np.cos(tw), np.sin(tw)]).astype(np.float32)
    return jnp.asarray(w1, BF16), jnp.asarray(w2, BF16), jnp.asarray(twiddle)


def fine_rows(groups, width):
    g = np.arange(groups)[:, None]
    i = np.arange(width)[None, :]
    fine = g * FD * (width - 1 - i) // (groups * (width - 1))
    hot = np.stack([fine == step for step in range(FD)])
    hot = hot.reshape(FD, groups, width // SIDE, SIDE).transpose(2, 0, 1, 3)
    return jnp.asarray(hot.reshape(-1, SIDE), BF16)


def front_kernel(scale, x_ref, halo_ref, proto_ref, w1_ref, w2_ref, tw_ref, p_ref, band_ref, carry):
    step = pl.program_id(0)

    @pl.when(step == 0)
    def _():
        carry[...] = halo_ref[...]
        band_ref[...] = jnp.zeros_like(band_ref)

    def frame(index):
        if index < 0:
            return carry[(index + 3) * SIDE : (index + 4) * SIDE]
        return x_ref[index * SIDE : (index + 1) * SIDE]

    total = None
    for s in range(0, SPB, 2):
        ys = []
        for k in (s, s + 1):
            acc = frame(k - 3) * proto_ref[0]
            for tap in range(1, 4):
                acc = acc + frame(k - 3 + tap) * proto_ref[tap]
            ys.append(acc.astype(BF16))
        a = jnp.dot(w1_ref[...], jnp.concatenate(ys, 1), preferred_element_type=F32)
        ts = []
        for m in range(2):
            re = a[:SIDE, m * SIDE : (m + 1) * SIDE]
            im = a[SIDE:, m * SIDE : (m + 1) * SIDE]
            t_re = re * tw_ref[0] - im * tw_ref[1]
            t_ni = im * tw_ref[0] + re * tw_ref[1]
            ts.append(jnp.concatenate([t_re.astype(BF16), t_ni.astype(BF16)], 1))
        c = jnp.dot(jnp.concatenate(ts, 0), w2_ref[...], preferred_element_type=F32)
        re, im = c[:, :SIDE], c[:, SIDE:]
        power = (re * re + im * im) * scale
        p_ref[s * SIDE : (s + 2) * SIDE] = power
        both = power[:SIDE] + power[SIDE:]
        total = both if total is None else total + both
    band_ref[...] += total
    carry[...] = x_ref[(SPB - 3) * SIDE :]


def front(x, halo, proto):
    taps, channels = proto.shape
    rows = x.shape[0]
    w1, w2, tw = tables(channels)
    full = lambda shape: pl.BlockSpec(shape, lambda i: (0,) * len(shape))
    return pl.pallas_call(
        functools.partial(front_kernel, 1.0 / (taps * channels)),
        grid=(rows // (SPB * SIDE),),
        in_specs=[
            pl.BlockSpec((SPB * SIDE, SIDE), lambda i: (i, 0)),
            full(halo.shape),
            full((taps, SIDE, SIDE)),
            full(w1.shape),
            full(w2.shape),
            full(tw.shape),
        ],
        out_specs=[pl.BlockSpec((SPB * SIDE, SIDE), lambda i: (i, 0)), full((SIDE, SIDE))],
        out_shape=[
            jax.ShapeDtypeStruct((rows, SIDE), F32),
            jax.ShapeDtypeStruct((SIDE, SIDE), F32),
        ],
        scratch_shapes=[pltpu.VMEM(halo.shape, F32)],
        compiler_params=pltpu.CompilerParams(vmem_limit_bytes=32 << 20),
        name="front",
    )(x, halo, proto.reshape(taps, SIDE, SIDE), w1, w2, tw)


def flat_kernel(spectra, groups, p_ref, band_ref, m_ref, tot_ref, inv):
    step = pl.program_id(0)

    @pl.when(step == 0)
    def _():
        inv[...] = 1.0 / (band_ref[...] * (1.0 / spectra) + 1e-06)
        tot_ref[...] = jnp.zeros_like(tot_ref)

    even = lax.broadcasted_iota(jnp.int32, (FD * groups, SIDE), 1) % 2 == 0
    for s in range(0, SPB, 2):
        flats = []
        for k in (s, s + 1):
            ratio = p_ref[k * SIDE : (k + 1) * SIDE] * inv[...]
            mean = jnp.sum(jnp.sum(ratio, 0, keepdims=True), 1, keepdims=True) * (1.0 / (SIDE * SIDE))
            flats.append((ratio - mean).astype(BF16))
        r = jnp.dot(m_ref[...], jnp.concatenate(flats, 1), preferred_element_type=F32)
        for m in range(2):
            part = r[:, m * SIDE : (m + 1) * SIDE]
            part = jnp.where(even, part[: FD * groups], part[FD * groups :])
            for d in range(FD):
                tot_ref[step * SPB + s + m + d] += part[d * groups : (d + 1) * groups]


def flat_sums(power, band, groups, spectra):
    spec = power.shape[0] // SIDE
    masks = fine_rows(groups, SIDE * SIDE // NBLK)
    full = lambda shape: pl.BlockSpec(shape, lambda i: (0,) * len(shape))
    out = (spec + FD - 1, groups, SIDE)
    return pl.pallas_call(
        functools.partial(flat_kernel, spectra, groups),
        grid=(spec // SPB,),
        in_specs=[
            pl.BlockSpec((SPB * SIDE, SIDE), lambda i: (i, 0)),
            full((SIDE, SIDE)),
            full(masks.shape),
        ],
        out_specs=full(out),
        out_shape=jax.ShapeDtypeStruct(out, F32),
        scratch_shapes=[pltpu.VMEM((SIDE, SIDE), F32)],
        compiler_params=pltpu.CompilerParams(vmem_limit_bytes=32 << 20),
        name="flatten",
    )(power, band, masks)


def trial_kernel(groups, spec, tail_ref, tot_ref, mask_ref, pack_ref, out_ref):
    quad = (MAXT + 1) * groups
    halo = MAXT * TT + WMAX - 1
    rows = spec + halo + 1
    ext = jnp.concatenate(
        [
            jnp.zeros((1, groups, SIDE), F32),
            tail_ref[:halo],
            tot_ref[: FD - 1] + tail_ref[halo:],
            tot_ref[FD - 1 : spec],
        ],
        0,
    ).reshape(rows * groups, SIDE)
    width = SIDE * SIDE // NBLK
    sub = ((ext + pltpu.roll(ext, SIDE - 1, 1)) * (1.0 / math.sqrt(width))).astype(BF16)
    prod = jnp.dot(sub, mask_ref[...], preferred_element_type=F32)
    lanes = prod.shape[1]
    prod = prod.reshape(rows, groups, lanes)
    lane = lax.broadcasted_iota(jnp.int32, (groups, lanes), 1)
    row = lax.broadcasted_iota(jnp.int32, (groups, lanes), 0)
    own = (lane // 4) % groups == row
    each = jnp.sum(jnp.where(own[None], prod, 0.0), 1)
    count = spec + TT
    dd = 0.0
    for value in range(MAXT + 1):
        start = (MAXT - value) * TT
        dd = dd + each[start : start + count, value * quad : (value + 1) * quad]
    dd = dd * (1.0 / math.sqrt(NBLK))
    wide = pack_ref.shape[1]
    if quad < wide:
        dd = jnp.concatenate([dd, jnp.zeros((count, wide - quad), F32)], 1)
    dd = jnp.concatenate([dd, jnp.zeros((2 * SIDE - count, wide), F32)], 0)
    out_ref[...] = jnp.dot(
        pack_ref[...], dd.T, preferred_element_type=F32, precision=lax.Precision.HIGHEST
    )


def trials_packed(tail, tot, mask, pack, groups, spec):
    return pl.pallas_call(
        functools.partial(trial_kernel, groups, spec),
        out_shape=jax.ShapeDtypeStruct((pack.shape[0], 2 * SIDE), F32),
        compiler_params=pltpu.CompilerParams(vmem_limit_bytes=48 << 20),
        name="trials",
    )(tail, tot, mask, pack)


def box_kernel(got_ref, weight_ref, out_ref):
    rows = got_ref.shape[0]
    got = got_ref[...]
    for n in range(rows // 8):
        part = got[n * 8 : (n + 1) * 8]
        acc = 0.0
        for lag in range(WMAX):
            moved = pltpu.roll(part, 2 * SIDE - (TT - lag), 1)[:, :SIDE]
            acc = acc + moved[:, None, :] * weight_ref[lag][None]
        out_ref[n * 8 : (n + 1) * 8] = acc


def boxcars(got, widths):
    lags = jnp.arange(WMAX, dtype=jnp.int32)
    weights = (lags[:, None] < widths[None, :]).astype(F32) / jnp.sqrt(widths.astype(F32))[None, :]
    weights = jnp.broadcast_to(weights[:, :, None], (WMAX, widths.shape[0], SIDE))
    return pl.pallas_call(
        box_kernel,
        out_shape=jax.ShapeDtypeStruct((got.shape[0], widths.shape[0], SIDE), F32),
        compiler_params=pltpu.CompilerParams(vmem_limit_bytes=32 << 20),
        name="boxcars",
    )(got, weights)


def slot_table(owners, owner_count, capacity):
    owner = owners[:, 0]
    index = jnp.arange(owner.shape[0], dtype=jnp.int32)
    same = owner[:, None] == owner[None, :]
    rank = jnp.sum((same & (index[None, :] < index[:, None])).astype(jnp.int32), 1)
    slot = owner * capacity + rank
    return slot[None, :] == jnp.arange(owner_count * capacity, dtype=jnp.int32)[:, None]


def shards(raw, proto, delays, widths, owners):
    taps, channels = proto.shape
    spec = raw.shape[1] // channels
    groups, trials, _ = delays.shape
    owner_count = lax.axis_size("dm")
    capacity = 2 * (groups // owner_count)
    spectra = spec * lax.axis_size("tm")
    halo = MAXT * TT + WMAX - 1

    before = shifted(raw[:, raw.shape[1] - (taps - 1) * channels :], "tm", 1)
    before = lax.optimization_barrier(before.astype(F32)).reshape(-1, SIDE)
    frames = lax.optimization_barrier(raw.astype(F32)).reshape(-1, SIDE)
    power, band = front(frames, before, proto)
    band = lax.psum(band, "tm")
    tot = flat_sums(power, band, groups, spectra)
    tail = shifted(tot[spec - halo :], "tm", 1)

    value = jnp.arange(MAXT + 1, dtype=jnp.int32)[:, None, None, None]
    hit = (delays[None] == value).reshape(-1, NBLK).T
    mask = jnp.stack([hit, jnp.zeros_like(hit)], 1).reshape(SIDE, -1).astype(BF16)
    table = slot_table(owners, owner_count, capacity)
    pack = table[:, None, :, None] & jnp.eye(trials, dtype=bool)[None, :, None, :]
    pack = pack.reshape(owner_count * capacity * trials, groups * trials).astype(F32)
    pack = jnp.pad(pack, ((0, 0), (0, -pack.shape[1] % SIDE)))

    packed = trials_packed(tail, tot, mask, pack, groups, spec)
    packed = packed.reshape(owner_count, capacity * trials, 2 * SIDE)
    got = lax.all_to_all(packed, "dm", split_axis=0, concat_axis=0, tiled=True)
    box = boxcars(got.reshape(-1, 2 * SIDE), widths)
    box = box.reshape(owner_count, capacity, 1, trials, widths.shape[0], spec)
    return jnp.transpose(box, (1, 0, 2, 3, 4, 5)).astype(BF16)


def solution(mesh):
    return jax.shard_map(
        shards,
        mesh=mesh,
        in_specs=(P(("group", "dm", "beam"), "tm"), P(), P(), P(), P()),
        out_specs=P("dm", "group", "beam", None, None, "tm"),
        check_vma=False,
    )
```

time: 274 us -> 95.7 us (0.35)
  other arithmetic: 137 us -> 12.1 us
  matrix products: 37.3 us -> 0 us
  local copies, waits for them, and re-layouts: 42.6 us -> 10.6 us
  Pallas kernels: 0 us -> 17.9 us
  loops' own time: 5.67 us -> 0 us
  waiting for transfers between devices: 25.2 us -> 29.1 us
    unnamed x2 -> x0, other arithmetic: 90.3 us -> none
    dot_general x63 -> x0, matrix products: 37.3 us -> none  [the longest x9 5.91 us: spectra_power(): jnp.einsum('kab,fa->kbf', frames_bf, cos_a, preferred_element_type=jnp.fl...]
    while x8 -> x0, other arithmetic: 24.1 us -> none
    pallas_call x0 -> x4, Pallas kernels: none -> 17.9 us  [the longest x1 11 us: front(): pl.pallas_call(functools.partial(front_kernel, 1.0 / (taps * channels)),...]
    psum x1, waiting for transfers between devices: 8.4 us -> 21.1 us  [shards(): band = lax.psum(band, 'tm')]
    dynamic_update_slice x8 -> x0, local copies, waits for them, and re-layouts: 8.56 us -> none  [blocked_power(): blocks = lax.map(block_power, jnp.arange(count // PFB_BLK, dtype=jnp.int32))]
    concatenate x4 -> x0, local copies, waits for them, and re-layouts: 8.35 us -> none  [shards(): jnp.concatenate([early_power, main_power], 1) / (band[:, None, :] + 1e-06)]
    reduce_sum x4 -> x1, other arithmetic: 9 us -> 0.92 us  [slot_table(): jnp.sum((same & (index[None, :] < index[:, None])).astype(jnp.int32), 1)]
  transfers between devices with their start and end apart: 4 -> 4, of which waited for: 4 -> 3; matrix products, arithmetic and copies ran while one was open for 6% -> 14% of each run, Pallas kernels for 0% -> 0%
where the time goes in v1:
time: 95.7 us; the launch traced here: 95.3 us
  waiting for transfers between devices  29.1 us (30%)
  Pallas kernels  17.9 us (19%)
  between operations  13.6 us (14%)
  other arithmetic  12.1 us (13%)
  starting transfers between devices  11.9 us (12%)
  local copies, waits for them, and re-layouts  10.6 us (11%)
    psum x1, waiting for transfers between devices, shards(): band = lax.psum(band, 'tm')  21.1 us
    pallas_call x1, Pallas kernels, front(): pl.pallas_call(functools.partial(front_kernel, 1.0 / (taps * channels)),...  11 us
    convert_element_type x1, other arithmetic, shards(): frames = lax.optimization_barrier(raw.astype(F32)).reshape(-1, SIDE)  10 us
    unnamed x19, local copies, waits for them, and re-layouts  7.5 us
    ppermute x2, starting transfers between devices, shifted(): lax.ppermute(value, axis, [(s, s + steps) for s in range(count - steps)])  6.95 us
    all_to_all x1, waiting for transfers between devices, shards(): got = lax.all_to_all(packed, 'dm', split_axis=0, concat_axis=0, tiled=True)  5.74 us
    all_to_all x1, starting transfers between devices, shards(): got = lax.all_to_all(packed, 'dm', split_axis=0, concat_axis=0, tiled=True)  4.97 us
    pallas_call x1, Pallas kernels, flat_sums(): pl.pallas_call(functools.partial(flat_kernel, spectra, groups), grid=(spe...  4.88 us
  transfers between devices with their start and end apart: 4, of which 3 were waited for; matrix products, arithmetic and copies ran while one was open for 14% of the time, Pallas kernels for 0%

profile of v1, /device:TPU:0, one launch (start us, length us, event | category | flops | bytes accessed | tf_op | source)
XLA Modules:
  0.0 95.3 jit_solution(14408550815167628315)
XLA Ops:
  6.5 0.0 all-reduce.4.cloned.1.call-start
  6.5 1.1 %slice.6 = bf16[1,49152]{1,0:T(2,128)(2,1)S(1)} slice(bf16[1,2097152]{1,0:T(2,128)(2,1)} %param.9), slice={[0:1], [2048000:2097152]} | slice | bytes 196608 | tf_op jit(solution)/shard_map/slice | solution.py:246
  7.7 4.9 %collective-permute-start = (bf16[1,49152]{1,0:T(2,128)(2,1)S(1)}, bf16[1,49152]{1,0:T(2,128)(2,1)S(1)}, u32[]{:S(2)}, u32[]{:S(2)}) collective-permute-start(bf16[1,49152]{1,0:T(2,128)(2,1)S(1)} %slice.6), channel_id=1, source_target_pairs={{0,2},{1,3},{4,6},{5,7},{8,10},{9,11},{12,14},{13,15},{16,18},{17,... | collective-permute-start | bytes 294920 | tf_op jit(solution)/shard_map/ppermute | solution.py:25
  12.6 0.1 eq.60
  12.7 0.9 convert_reduce_fusion
  13.6 0.7 multiply_add_fusion
  14.2 0.1 iota_compare_fusion.1
  14.3 0.7 eq.57
  15.0 0.1 compare_bitcast_fusion
  15.1 0.1 broadcast_and_fusion
  15.2 0.0 copy-start.7
  15.2 0.0 copy-start.2
  15.3 0.0 copy-start.3
  15.3 0.0 copy-start.4
  15.3 10.0 %convert_element_type.39 = f32[1,2097152]{1,0:T(1,128)S(1)} convert(bf16[1,2097152]{1,0:T(2,128)(2,1)} %param.9) | non-fusion elementwise | flops 2097152 | bytes 12582912 | tf_op jit(solution)/shard_map/convert_element_type | solution.py:248
  25.3 0.0 copy-start.8
  25.3 0.0 copy-start.6
  25.4 0.0 copy-done.7
  25.4 0.0 collective-permute-done
  25.4 0.2 convert_element_type.40
  25.6 0.0 copy-done.2
  25.6 0.0 copy-done.3
  25.6 0.0 copy-done.4
  25.7 11.0 %front.1 = (f32[16384,128]{1,0:T(8,128)S(1)}, f32[128,128]{1,0:T(8,128)}) custom-call(f32[16384,128]{1,0:T(8,128)S(1)} %bitcast.23, f32[384,128]{1,0:T(8,128)S(1)} %bitcast.25, f32[4,128,128]{2,1,0:T(8,128)S(1)} %bitcast.24, bf16[256,128]{1,0:T(8,128)(2,1)S(1)} %copy-done.4, bf16[256,256]{1,0:T(8,128)(2,1)S(1)} %copy-done.2, f32[2,128,128]{2,1,0:T(8,128)S(1)} %copy-done.3), custom_call_target="tpu_custom_call" | custom-call | tf_op jit(solution)/shard_map/front/pallas_call | solution.py:92
  36.7 0.0 copy-start
  36.7 3.2 %copy-done = f32[16384,128]{1,0:T(8,128)} copy-done((f32[16384,128]{1,0:T(8,128)}, f32[16384,128]{1,0:T(8,128)S(1)}, u32[]{:S(2)}) %copy-start) | copy-done | bytes 8388632
  39.9 0.0 all-reduce.4.cloned.1.call-update
  39.9 0.0 copy-done.8
  39.9 0.1 copy.16
  40.0 21.1 %all-reduce.4.cloned.1.call-done.band_ref = f32[128,128]{1,0:T(8,128)} async-done(((f32[128,128]{1,0:T(8,128)}), f32[128,128]{1,0:T(8,128)}) %all-reduce.4.cloned.1.call-update) | async-done | bytes 65552 | tf_op jit(solution)/shard_map/psum | solution.py:250
  61.2 0.0 copy-done.6
  61.2 0.0 copy-start.1
  61.2 3.4 %copy-done.1 = f32[16384,128]{1,0:T(8,128)S(1)} copy-done((f32[16384,128]{1,0:T(8,128)S(1)}, f32[16384,128]{1,0:T(8,128)}, u32[]{:S(2)}) %copy-start.1) | copy-done | bytes 8388632
  64.6 0.0 copy-start.5
  64.6 0.8 copy-done.5
  65.4 4.9 %flatten.1.tot_ref = f32[131,8,128]{2,1,0:T(8,128)S(1)} custom-call(f32[16384,128]{1,0:T(8,128)S(1)} %copy-done.1, f32[128,128]{1,0:T(8,128)S(1)} %copy-done.5, bf16[64,128]{1,0:T(8,128)(2,1)S(1)} %copy-done.6), custom_call_target="tpu_custom_call" | custom-call | tf_op jit(solution)/shard_map/flatten/pallas_call | solution.py:142
  70.3 2.1 %collective-permute-start.1 = (f32[34,8,128]{2,1,0:T(8,128)S(1)}, f32[34,8,128]{2,1,0:T(8,128)S(1)}, u32[]{:S(2)}, u32[]{:S(2)}) collective-permute-start(f32[34,8,128]{2,1,0:T(8,128)S(1)} %slice.8), channel_id=1, source_target_pairs={{0,2},{1,3},{4,6},{5,7},{8,10},{9,11},{12,14},{13,15},{16,18},{17,... | collective-permute-start | bytes 417800 | tf_op jit(solution)/shard_map/ppermute | solution.py:25
  72.5 0.2 convert_element_type.44
  72.6 0.1 copy.18
  72.8 2.2 %collective-permute-done.1.tail_ref = f32[34,8,128]{2,1,0:T(8,128)S(1)} collective-permute-done((f32[34,8,128]{2,1,0:T(8,128)S(1)}, f32[34,8,128]{2,1,0:T(8,128)S(1)}, u32[]{:S(2)}, u32[]{:S(2)}) %collective-permute-start.1) | collective-permute-done | bytes 139296 | tf_op jit(solution)/shard_map/ppermute | solution.py:25
  75.0 1.6 %trials.1 = f32[64,256]{1,0:T(8,128)} custom-call(f32[34,8,128]{2,1,0:T(8,128)S(1)} %collective-permute-done.1.tail_ref, f32[131,8,128]{2,1,0:T(8,128)S(1)} %flatten.1.tot_ref, bf16[128,128]{1,0:T(8,128)(2,1)S(1)} %bitcast.27, f32[64,128]{1,0:T(8,128)S(1)} %pad_convert_fusion.1.pack_ref), custom_call_target="tpu_custom_call" | custom-call | tf_op jit(solution)/shard_map/trials/pallas_call | solution.py:196
  76.6 5.0 %all-to-all-start = ((f32[4,16,256]{2,1,0:T(8,128)}), f32[4,16,256]{2,1,0:T(8,128)S(1)}, u32[]{:S(2)}, u32[]{:S(2)}) async-start(f32[4,16,256]{2,1,0:T(8,128)} %bitcast.7), calls=%async_computation | async-start | bytes 131072 | tf_op jit(solution)/shard_map/all_to_all | solution.py:264
  81.6 5.7 %all-to-all-done = f32[4,16,256]{2,1,0:T(8,128)S(1)} async-done(((f32[4,16,256]{2,1,0:T(8,128)}), f32[4,16,256]{2,1,0:T(8,128)S(1)}, u32[]{:S(2)}, u32[]{:S(2)}) %all-to-all-start) | async-done | bytes 65568 | tf_op jit(solution)/shard_map/all_to_all | solution.py:264
  87.3 0.1 broadcast_in_dim.2.weight_ref
  87.4 0.4 boxcars.1
  87.8 0.7 copy.24
  (10 shorter events, 0.1 us)
Async XLA Ops:
  6.5 54.6 %all-reduce.4.cloned.1.call-start = ((), (), s32[]{:S(2)}) async-start(), calls=%async_computation.1 | async-start | bytes 131072 | tf_op jit(solution)/shard_map/psum | solution.py:250
  7.7 17.7 %collective-permute-start = (bf16[1,49152]{1,0:T(2,128)(2,1)S(1)}, bf16[1,49152]{1,0:T(2,128)(2,1)S(1)}, u32[]{:S(2)}, u32[]{:S(2)}) collective-permute-start(bf16[1,49152]{1,0:T(2,128)(2,1)S(1)} %slice.6), channel_id=1, source_target_pairs={{0,2},{1,3},{4,6},{5,7},{8,10},{9,11},{12,14},{13,15},{16,18},{17,... | collective-permute-start | bytes 294920 | tf_op jit(solution)/shard_map/ppermute | solution.py:25
  15.2 10.1 %copy-start.7 = (f32[4,16384]{1,0:T(4,128)S(1)}, f32[4,16384]{1,0:T(4,128)}, u32[]{:S(2)}) copy-start(f32[4,16384]{1,0:T(4,128)} %param.10) | copy-start | bytes 786436
  15.2 10.4 %copy-start.2 = (bf16[256,256]{1,0:T(8,128)(2,1)S(1)}, bf16[256,256]{1,0:T(8,128)(2,1)}, u32[]{:S(2)}) copy-start(bf16[256,256]{1,0:T(8,128)(2,1)} %constant.17.clone.w2_ref) | copy-start | bytes 393220
  15.3 10.4 %copy-start.3 = (f32[2,128,128]{2,1,0:T(8,128)S(1)}, f32[2,128,128]{2,1,0:T(8,128)}, u32[]{:S(2)}) copy-start(f32[2,128,128]{2,1,0:T(8,128)} %constant.18.clone.tw_ref) | copy-start | bytes 393220
  15.3 10.4 %copy-start.4 = (bf16[256,128]{1,0:T(8,128)(2,1)S(1)}, bf16[256,128]{1,0:T(8,128)(2,1)}, u32[]{:S(2)}) copy-start(bf16[256,128]{1,0:T(8,128)(2,1)} %constant.16.clone.w1_ref) | copy-start | bytes 196612
  25.3 14.6 %copy-start.8 = (s32[8]{0:T(128)S(1)}, s32[8]{0:T(128)}, u32[]{:S(2)}) copy-start(s32[8]{0:T(128)} %param.12) | copy-start | bytes 100
  25.3 35.8 %copy-start.6 = (bf16[64,128]{1,0:T(8,128)(2,1)S(1)}, bf16[64,128]{1,0:T(8,128)(2,1)}, u32[]{:S(2)}) copy-start(bf16[64,128]{1,0:T(8,128)(2,1)} %constant.19.clone.m_ref) | copy-start | bytes 49156
  36.7 3.2 %copy-start = (f32[16384,128]{1,0:T(8,128)}, f32[16384,128]{1,0:T(8,128)S(1)}, u32[]{:S(2)}) copy-start(f32[16384,128]{1,0:T(8,128)S(1)} %get-tuple-element.7.p_ref) | copy-start | bytes 25165828
  61.2 3.4 %copy-start.1 = (f32[16384,128]{1,0:T(8,128)S(1)}, f32[16384,128]{1,0:T(8,128)}, u32[]{:S(2)}) copy-start(f32[16384,128]{1,0:T(8,128)} %copy-done) | copy-start | bytes 25165828
  64.6 0.8 copy-start.5
  70.3 4.7 %collective-permute-start.1 = (f32[34,8,128]{2,1,0:T(8,128)S(1)}, f32[34,8,128]{2,1,0:T(8,128)S(1)}, u32[]{:S(2)}, u32[]{:S(2)}) collective-permute-start(f32[34,8,128]{2,1,0:T(8,128)S(1)} %slice.8), channel_id=1, source_target_pairs={{0,2},{1,3},{4,6},{5,7},{8,10},{9,11},{12,14},{13,15},{16,18},{17,... | collective-permute-start | bytes 417800 | tf_op jit(solution)/shard_map/ppermute | solution.py:25
  76.6 10.7 %all-to-all-start = ((f32[4,16,256]{2,1,0:T(8,128)}), f32[4,16,256]{2,1,0:T(8,128)S(1)}, u32[]{:S(2)}, u32[]{:S(2)}) async-start(f32[4,16,256]{2,1,0:T(8,128)} %bitcast.7), calls=%async_computation | async-start | bytes 131072 | tf_op jit(solution)/shard_map/all_to_all | solution.py:264
Sparse Core Ops, SparseCore 0:
  40.0 21.0 all-reduce.3

commit v2 on v1

v2 whole, which is shorter than its diff:
```python
import functools
import math

import jax
import jax.numpy as jnp
import numpy as np
from jax import lax
from jax.experimental import pallas as pl
from jax.experimental.pallas import tpu as pltpu
from jax.sharding import PartitionSpec as P

SIDE = 128
NBLK = 64
FD = 4
TT = 8
MAXT = 3
WMAX = 8
SPB = 8
MESH = pl.DeviceIdType.MESH
F32 = jnp.float32
BF16 = jnp.bfloat16


def shifted(value, axis, steps):
    count = lax.axis_size(axis)
    return lax.ppermute(value, axis, [(s, s + steps) for s in range(count - steps)])


def tables(channels):
    i = np.arange(SIDE)
    ang = (i[:, None] * i[None, :] % SIDE) * (2.0 * math.pi / SIDE)
    c, s = np.cos(ang), np.sin(ang)
    w1 = np.concatenate([c, s], 0)
    w2 = np.block([[c, -s], [-s, -c]])
    tw = (i[:, None] * i[None, :] % channels) * (2.0 * math.pi / channels)
    twiddle = np.stack([np.cos(tw), np.sin(tw)]).astype(np.float32)
    return jnp.asarray(w1, BF16), jnp.asarray(w2, BF16), jnp.asarray(twiddle)


def fine_rows(groups, width):
    g = np.arange(groups)[:, None]
    i = np.arange(width)[None, :]
    fine = g * FD * (width - 1 - i) // (groups * (width - 1))
    hot = np.stack([fine == step for step in range(FD)])
    hot = hot.reshape(FD, groups, width // SIDE, SIDE).transpose(2, 0, 1, 3)
    return jnp.asarray(hot.reshape(-1, SIDE), BF16)


def front_kernel(scale, x_ref, halo_ref, proto_ref, w1_ref, w2_ref, tw_ref, p_ref, band_ref, window):
    step = pl.program_id(0)

    def unfold(ref, index):
        line = ref[:, index * SIDE * SIDE : (index + 1) * SIDE * SIDE]
        return line.astype(F32).reshape(SIDE, SIDE)

    @pl.when(step == 0)
    def _():
        for k in range(3):
            window[k * SIDE : (k + 1) * SIDE] = unfold(halo_ref, k)
        band_ref[...] = jnp.zeros_like(band_ref)

    def frame(index):
        return window[(index + 3) * SIDE : (index + 4) * SIDE]

    total = None
    for s in range(0, SPB, 2):
        for k in (s, s + 1):
            window[(k + 3) * SIDE : (k + 4) * SIDE] = unfold(x_ref, k)
        ys = []
        for k in (s, s + 1):
            acc = frame(k - 3) * proto_ref[0]
            for tap in range(1, 4):
                acc = acc + frame(k - 3 + tap) * proto_ref[tap]
            ys.append(acc.astype(BF16))
        a = jnp.dot(w1_ref[...], jnp.concatenate(ys, 1), preferred_element_type=F32)
        ts = []
        for m in range(2):
            re = a[:SIDE, m * SIDE : (m + 1) * SIDE]
            im = a[SIDE:, m * SIDE : (m + 1) * SIDE]
            t_re = re * tw_ref[0] - im * tw_ref[1]
            t_ni = im * tw_ref[0] + re * tw_ref[1]
            ts.append(jnp.concatenate([t_re.astype(BF16), t_ni.astype(BF16)], 1))
        c = jnp.dot(jnp.concatenate(ts, 0), w2_ref[...], preferred_element_type=F32)
        re, im = c[:, :SIDE], c[:, SIDE:]
        power = (re * re + im * im) * scale
        p_ref[s * SIDE : (s + 2) * SIDE] = power
        both = power[:SIDE] + power[SIDE:]
        total = both if total is None else total + both
    band_ref[...] += total
    window[: 3 * SIDE] = window[SPB * SIDE :]


def front(x, halo, proto):
    taps, channels = proto.shape
    rows = x.shape[1] // SIDE
    w1, w2, tw = tables(channels)
    full = lambda shape: pl.BlockSpec(shape, lambda i: (0,) * len(shape))
    return pl.pallas_call(
        functools.partial(front_kernel, 1.0 / (taps * channels)),
        grid=(rows // (SPB * SIDE),),
        in_specs=[
            pl.BlockSpec((1, SPB * SIDE * SIDE), lambda i: (0, i)),
            full(halo.shape),
            full((taps, SIDE, SIDE)),
            full(w1.shape),
            full(w2.shape),
            full(tw.shape),
        ],
        out_specs=[pl.BlockSpec((SPB * SIDE, SIDE), lambda i: (i, 0)), full((SIDE, SIDE))],
        out_shape=[
            jax.ShapeDtypeStruct((rows, SIDE), F32),
            jax.ShapeDtypeStruct((SIDE, SIDE), F32),
        ],
        scratch_shapes=[pltpu.VMEM(((SPB + 3) * SIDE, SIDE), F32)],
        compiler_params=pltpu.CompilerParams(vmem_limit_bytes=40 << 20),
        name="front",
    )(x, halo, proto.reshape(taps, SIDE, SIDE), w1, w2, tw)


def search_kernel(
    sizes, p_ref, band_ref, m_ref, mask_ref, pack_ref, weight_ref, out_ref,
    bands, inv, tot, tail, send, got, band_send, band_recv, tail_send, tail_recv, own_send, own_recv,
):
    spectra, spec, groups, slabs, owner_count, axes = sizes
    halo = MAXT * TT + WMAX - 1
    quad = (MAXT + 1) * groups
    tm, dm = lax.axis_index("tm"), lax.axis_index("dm")

    def peer(axis, shift):
        place = {name: lax.axis_index(name) for name in axes}
        place[axis] = lax.rem(place[axis] + shift, lax.axis_size(axis))
        return tuple(place[name] for name in axes)

    barrier = pltpu.get_barrier_semaphore()
    for off in range(1, slabs):
        pl.semaphore_signal(barrier, inc=1, device_id=peer("tm", off), device_id_type=MESH)
    for off in range(1, owner_count):
        pl.semaphore_signal(barrier, inc=1, device_id=peer("dm", off), device_id_type=MESH)
    pl.semaphore_wait(barrier, slabs + owner_count - 2)

    copies = []
    for off in range(1, slabs):
        copy = pltpu.make_async_remote_copy(
            src_ref=band_ref,
            dst_ref=bands.at[off - 1],
            send_sem=band_send.at[off - 1],
            recv_sem=band_recv.at[off - 1],
            device_id=peer("tm", off),
            device_id_type=MESH,
        )
        copy.start()
        copies.append(copy)
    tot[...] = jnp.zeros_like(tot)
    band = band_ref[...]
    for off in range(1, slabs):
        copies[off - 1].wait()
        band = band + bands[off - 1]
    inv[...] = 1.0 / (band * (1.0 / spectra) + 1e-06)

    even = lax.broadcasted_iota(jnp.int32, (FD * groups, SIDE), 1) % 2 == 0

    def block(step, carry):
        for s in range(0, SPB, 2):
            flats = []
            for k in (s, s + 1):
                start = pl.multiple_of((step * SPB + k) * SIDE, SIDE)
                ratio = p_ref[pl.ds(start, SIDE)] * inv[...]
                mean = jnp.sum(jnp.sum(ratio, 0, keepdims=True), 1, keepdims=True)
                flats.append((ratio - mean * (1.0 / (SIDE * SIDE))).astype(BF16))
            r = jnp.dot(m_ref[...], jnp.concatenate(flats, 1), preferred_element_type=F32)
            for m in range(2):
                part = r[:, m * SIDE : (m + 1) * SIDE]
                part = jnp.where(even, part[: FD * groups], part[FD * groups :])
                for d in range(FD):
                    tot[step * SPB + s + m + d] += part[d * groups : (d + 1) * groups]
        return carry

    blocks = spec // SPB
    last = -(-(halo + FD - 1) // SPB)
    lax.fori_loop(blocks - last, blocks, block, 0)
    if slabs > 1:
        tail_copy = pltpu.make_async_remote_copy(
            src_ref=tot.at[pl.ds(spec - halo, halo + FD - 1)],
            dst_ref=tail,
            send_sem=tail_send,
            recv_sem=tail_recv,
            device_id=peer("tm", 1),
            device_id_type=MESH,
        )
        tail_copy.start()
        lax.fori_loop(0, blocks - last, block, 0)
        tail_copy.wait()
        before = jnp.where(tm > 0, tail[...], 0.0)
    else:
        lax.fori_loop(0, blocks - last, block, 0)
        before = jnp.zeros(tail.shape, F32)

    rows = spec + halo + 1
    ext = jnp.concatenate(
        [
            jnp.zeros((1, groups, SIDE), F32),
            before[:halo],
            tot[: FD - 1] + before[halo:],
            tot[FD - 1 : spec],
        ],
        0,
    ).reshape(rows * groups, SIDE)
    width = SIDE * SIDE // NBLK
    sub = ((ext + pltpu.roll(ext, SIDE - 1, 1)) * (1.0 / math.sqrt(width))).astype(BF16)
    prod = jnp.dot(sub, mask_ref[...], preferred_element_type=F32)
    lanes = prod.shape[1]
    prod = prod.reshape(rows, groups, lanes)
    lane = lax.broadcasted_iota(jnp.int32, (groups, lanes), 1)
    row = lax.broadcasted_iota(jnp.int32, (groups, lanes), 0)
    own = (lane // 4) % groups == row
    each = jnp.sum(jnp.where(own[None], prod, 0.0), 1)
    count = spec + TT
    dd = 0.0
    for value in range(MAXT + 1):
        start = (MAXT - value) * TT
        dd = dd + each[start : start + count, value * quad : (value + 1) * quad]
    dd = dd * (1.0 / math.sqrt(NBLK))
    wide = pack_ref.shape[1]
    if quad < wide:
        dd = jnp.concatenate([dd, jnp.zeros((count, wide - quad), F32)], 1)
    dd = jnp.concatenate([dd, jnp.zeros((2 * SIDE - count, wide), F32)], 0)
    packed = jnp.dot(
        pack_ref[...], dd.T, preferred_element_type=F32, precision=lax.Precision.HIGHEST
    )
    send[...] = packed.reshape(send.shape)

    copies = []
    for off in range(1, owner_count):
        copy = pltpu.make_async_remote_copy(
            src_ref=send.at[lax.rem(dm + off, owner_count)],
            dst_ref=got.at[dm],
            send_sem=own_send.at[off - 1],
            recv_sem=own_recv.at[off - 1],
            device_id=peer("dm", off),
            device_id_type=MESH,
        )
        copy.start()
        copies.append(copy)
    got[dm] = send[dm]
    for copy in copies:
        copy.wait()

    slots, trials = out_ref.shape[0], out_ref.shape[2]
    for d in range(owner_count):
        part = got[d]
        acc = 0.0
        for lag in range(WMAX):
            moved = pltpu.roll(part, 2 * SIDE - (TT - lag), 1)[:, :SIDE]
            acc = acc + moved[:, None, :] * weight_ref[lag][None]
        for s in range(slots):
            out_ref[s, d] = acc[s * trials : (s + 1) * trials]


def search(power, band, mask, pack, widths, groups, capacity, trials, axes):
    slabs, owner_count = lax.axis_size("tm"), lax.axis_size("dm")
    spec = power.shape[0] // SIDE
    halo = MAXT * TT + WMAX - 1
    masks = fine_rows(groups, SIDE * SIDE // NBLK)
    lags = jnp.arange(WMAX, dtype=jnp.int32)
    weights = (lags[:, None] < widths[None, :]).astype(F32) / jnp.sqrt(widths.astype(F32))[None, :]
    weights = jnp.broadcast_to(weights[:, :, None], (WMAX, widths.shape[0], SIDE))
    sizes = (spec * slabs, spec, groups, slabs, owner_count, axes)
    block = pltpu.VMEM((owner_count, capacity * trials, 2 * SIDE), F32)
    sems = lambda n: pltpu.SemaphoreType.DMA((max(n, 1),))
    return pl.pallas_call(
        functools.partial(search_kernel, sizes),
        in_specs=[pl.BlockSpec(memory_space=pltpu.VMEM)] * 6,
        out_specs=pl.BlockSpec(memory_space=pltpu.VMEM),
        out_shape=jax.ShapeDtypeStruct(
            (capacity, owner_count, trials, widths.shape[0], spec), F32
        ),
        scratch_shapes=[
            pltpu.VMEM((max(slabs - 1, 1), SIDE, SIDE), F32),
            pltpu.VMEM((SIDE, SIDE), F32),
            pltpu.VMEM((spec + FD - 1, groups, SIDE), F32),
            pltpu.VMEM((halo + FD - 1, groups, SIDE), F32),
            block,
            block,
            sems(slabs - 1),
            sems(slabs - 1),
            pltpu.SemaphoreType.DMA,
            pltpu.SemaphoreType.DMA,
            sems(owner_count - 1),
            sems(owner_count - 1),
        ],
        compiler_params=pltpu.CompilerParams(
            vmem_limit_bytes=40 << 20, collective_id=0, has_side_effects=True
        ),
        name="search",
    )(power, band, masks, mask, pack, weights)


def slot_table(owners, owner_count, capacity):
    owner = owners[:, 0]
    index = jnp.arange(owner.shape[0], dtype=jnp.int32)
    same = owner[:, None] == owner[None, :]
    rank = jnp.sum((same & (index[None, :] < index[:, None])).astype(jnp.int32), 1)
    slot = owner * capacity + rank
    return slot[None, :] == jnp.arange(owner_count * capacity, dtype=jnp.int32)[:, None]


def shards(axes, raw, proto, delays, widths, owners):
    taps, channels = proto.shape
    spec = raw.shape[1] // channels
    groups, trials, _ = delays.shape
    owner_count = lax.axis_size("dm")
    capacity = 2 * (groups // owner_count)

    before = shifted(raw[:, raw.shape[1] - (taps - 1) * channels :], "tm", 1)
    power, band = front(raw, before, proto)

    value = jnp.arange(MAXT + 1, dtype=jnp.int32)[:, None, None, None]
    hit = (delays[None] == value).reshape(-1, NBLK).T
    mask = jnp.stack([hit, jnp.zeros_like(hit)], 1).reshape(SIDE, -1).astype(BF16)
    table = slot_table(owners, owner_count, capacity)
    pack = table[:, None, :, None] & jnp.eye(trials, dtype=bool)[None, :, None, :]
    pack = pack.reshape(owner_count * capacity * trials, groups * trials).astype(F32)
    pack = jnp.pad(pack, ((0, 0), (0, -pack.shape[1] % SIDE)))

    box = search(power, band, mask, pack, widths, groups, capacity, trials, axes)
    return box.astype(BF16)[:, :, None]


def solution(mesh):
    return jax.shard_map(
        functools.partial(shards, mesh.axis_names),
        mesh=mesh,
        in_specs=(P(("group", "dm", "beam"), "tm"), P(), P(), P(), P()),
        out_specs=P("dm", "group", "beam", None, None, "tm"),
        check_vma=False,
    )
```

time: 95.7 us -> 46.7 us (0.49)
  waiting for transfers between devices: 29.1 us -> 0.01 us
  between operations: 13.6 us -> 0.11 us
  Pallas kernels: 17.9 us -> 31.2 us
  other arithmetic: 12.1 us -> 3.86 us
  starting transfers between devices: 11.9 us -> 4.85 us
  local copies, waits for them, and re-layouts: 10.6 us -> 6.07 us
    psum x1 -> x0, waiting for transfers between devices: 21.1 us -> none  [shards(): band = lax.psum(band, 'tm')]
    convert_element_type x3 -> x0, other arithmetic: 10.3 us -> none  [the longest x1 10 us: shards(): frames = lax.optimization_barrier(raw.astype(F32)).reshape(-1, SIDE)]
    pallas_call x3 -> x1, Pallas kernels: 6.9 us -> 16.7 us  [search(): pl.pallas_call(functools.partial(search_kernel, sizes), in_specs=[pl.Bloc...]
    all_to_all x1 -> x0, waiting for transfers between devices: 5.74 us -> none  [shards(): got = lax.all_to_all(packed, 'dm', split_axis=0, concat_axis=0, tiled=True)]
    all_to_all x1 -> x0, starting transfers between devices: 4.97 us -> none  [shards(): got = lax.all_to_all(packed, 'dm', split_axis=0, concat_axis=0, tiled=True)]
    unnamed x19 -> x9, local copies, waits for them, and re-layouts: 7.5 us -> 3.62 us
    pallas_call x1, Pallas kernels: 11 us -> 14.4 us  [front(): pl.pallas_call(functools.partial(front_kernel, 1.0 / (taps * channels)),...]
    ppermute x2 -> x1, waiting for transfers between devices: 2.23 us -> 0.01 us  [shifted(): lax.ppermute(value, axis, [(s, s + steps) for s in range(count - steps)])]
  transfers between devices with their start and end apart: 4 -> 1, of which waited for: 3 -> 0; matrix products, arithmetic and copies ran while one was open for 14% -> 12% of each run, Pallas kernels for 0% -> 0%
where the time goes in v2:
time: 46.7 us; the launch traced here: 46 us
  Pallas kernels  31.2 us (67%)
  local copies, waits for them, and re-layouts  6.07 us (13%)
  starting transfers between devices  4.85 us (10%)
  other arithmetic  3.86 us (8%)
    pallas_call x1, Pallas kernels, search(): pl.pallas_call(functools.partial(search_kernel, sizes), in_specs=[pl.Bloc...  16.7 us
    pallas_call x1, Pallas kernels, front(): pl.pallas_call(functools.partial(front_kernel, 1.0 / (taps * channels)),...  14.4 us
    ppermute x1, starting transfers between devices, shifted(): lax.ppermute(value, axis, [(s, s + steps) for s in range(count - steps)])  4.85 us
    unnamed x9, local copies, waits for them, and re-layouts  3.62 us
    slice x1, local copies, waits for them, and re-layouts, shards(): before = shifted(raw[:, raw.shape[1] - (taps - 1) * channels:], 'tm', 1)  1.14 us
  transfers between devices with their start and end apart: 1, of which 0 were waited for; matrix products, arithmetic and copies ran while one was open for 12% of the time, Pallas kernels for 0%

profile of v2, /device:TPU:0, one launch (start us, length us, event | category | flops | bytes accessed | tf_op | source)
XLA Modules:
  0.0 46.0 jit_solution(13941924423230285032)
XLA Ops:
  0.0 0.0 copy-start.3
  0.0 1.1 %slice.3 = bf16[1,49152]{1,0:T(2,128)(2,1)S(1)} slice(bf16[1,2097152]{1,0:T(2,128)(2,1)} %x_ref.1), slice={[0:1], [2048000:2097152]} | slice | bytes 196608 | tf_op jit(solution)/shard_map/slice | solution.py:314
  1.1 4.9 %collective-permute-start = (bf16[1,49152]{1,0:T(2,128)(2,1)S(1)}, bf16[1,49152]{1,0:T(2,128)(2,1)S(1)}, u32[]{:S(2)}, u32[]{:S(2)}) collective-permute-start(bf16[1,49152]{1,0:T(2,128)(2,1)S(1)} %slice.3), channel_id=1, source_target_pairs={{0,2},{1,3},{4,6},{5,7},{8,10},{9,11},{12,14},{13,15},{16,18},{17,... | collective-permute-start | bytes 294920 | tf_op jit(solution)/shard_map/ppermute | solution.py:26
  6.0 1.0 %copy.22 = f32[1,4,128,128]{3,2,1,0:T(8,128)S(1)} copy(f32[1,4,128,128]{3,1,2,0:T(4,128)} %bitcast.22) | data formatting | bytes 524288
  7.0 0.1 eq.60
  7.1 0.7 %eq.57 = s32[4,8,4,64]{3,2,1,0:T(4,128)S(1)} broadcast(s32[8,4,64]{2,1,0:T(4,128)} %param.11), dimensions={1,2,3} | broadcast | bytes 40960 | tf_op jit(solution)/shard_map/eq | solution.py:318
  7.8 0.1 compare_bitcast_fusion
  7.9 0.1 copy.16
  8.1 0.9 %convert_reduce_fusion = s32[8]{0:T(128)S(1)} fusion(s32[8]{0:T(128)} %bitcast.24), kind=kLoop, calls=%fused_computation.9 | loop fusion | flops 312 | bytes 64 | tf_op jit(solution)/shard_map/reduce_sum | solution.py:302
  9.0 0.7 %multiply_add_fusion = s32[8]{0:T(128)S(1)} fusion(s32[8]{0:T(128)S(1)} %convert_reduce_fusion, s32[8,1]{0,1:T(1,128)} %param.13), kind=kLoop, calls=%fused_computation.14 | loop fusion | flops 16 | bytes 96 | tf_op jit(solution)/shard_map/add | solution.py:303
  9.7 0.1 iota_compare_fusion.1
  9.7 0.1 broadcast_and_fusion
  9.8 0.2 convert_element_type.30
  10.0 0.1 copy.18
  10.1 0.7 %convert_sqrt_fusion = f32[8]{0:T(128)S(1)} fusion(s32[8]{0:T(128)} %param.12), kind=kLoop, calls=%fused_computation.13 | loop fusion | flops 8 | bytes 64 | tf_op jit(solution)/shard_map/sqrt | solution.py:265
  10.8 0.7 %convert_divide_fusion = f32[8,8]{1,0:T(8,128)S(1)} fusion(f32[8]{0:T(128)S(1)} %convert_sqrt_fusion, s32[8]{0:T(128)} %param.12), kind=kLoop, calls=%fused_computation.6 | loop fusion | flops 192 | bytes 320 | tf_op jit(solution)/shard_map/div | solution.py:265
  11.5 0.0 collective-permute-done.halo_ref
  11.5 0.0 copy-start
  11.5 0.9 %copy-done = bf16[256,256]{1,0:T(8,128)(2,1)S(1)} copy-done((bf16[256,256]{1,0:T(8,128)(2,1)S(1)}, bf16[256,256]{1,0:T(8,128)(2,1)}, u32[]{:S(2)}) %copy-start) | copy-done | bytes 131096
  12.4 0.0 copy-start.1
  12.4 0.9 %copy-done.1 = f32[2,128,128]{2,1,0:T(8,128)S(1)} copy-done((f32[2,128,128]{2,1,0:T(8,128)S(1)}, f32[2,128,128]{2,1,0:T(8,128)}, u32[]{:S(2)}) %copy-start.1) | copy-done | bytes 131096
  13.3 0.0 copy-start.2
  13.3 0.8 %copy-done.2 = bf16[256,128]{1,0:T(8,128)(2,1)S(1)} copy-done((bf16[256,128]{1,0:T(8,128)(2,1)S(1)}, bf16[256,128]{1,0:T(8,128)(2,1)}, u32[]{:S(2)}) %copy-start.2) | copy-done | bytes 65560
  14.1 14.4 %front.1 = (f32[16384,128]{1,0:T(8,128)S(1)}, f32[128,128]{1,0:T(8,128)S(1)}) custom-call(bf16[1,2097152]{1,0:T(2,128)(2,1)} %x_ref.1, bf16[1,49152]{1,0:T(2,128)(2,1)S(1)} %collective-permute-done.halo_ref, f32[4,128,128]{2,1,0:T(8,128)S(1)} %bitcast.19, bf16[256,128]{1,0:T(8,128)(2,1)S(1)} %copy-done.2, bf16[256,256]{1,0:T(8,128)(2,1)S(1)} %copy-done, ...), custom_call_target="tpu_custom_call" | custom-call | tf_op jit(solution)/shard_map/front/pallas_call | solution.py:98
  28.6 0.1 broadcast_in_dim.4.weight_ref
  28.6 0.0 copy-done.3
  28.6 16.7 %search.1 = f32[4,4,4,8,128]{4,3,2,1,0:T(8,128)S(1)} custom-call(f32[16384,128]{1,0:T(8,128)S(1)} %get-tuple-element.7.p_ref, f32[128,128]{1,0:T(8,128)S(1)} %get-tuple-element.8.band_ref, bf16[64,128]{1,0:T(8,128)(2,1)S(1)} %copy-done.3, bf16[128,128]{1,0:T(8,128)(2,1)S(1)} %bitcast.20, f32[64,128]{1,0:T(8,128)S(1)} %pad_convert_fusion.1.pack_ref, ...), custom_call_target="tpu_custom_call" | custom-call | tf_op jit(solution)/shard_map/search/pallas_call | solution.py:270
  45.4 0.7 %convert_bitcast_fusion = bf16[4,4,1,4,8,128]{5,4,3,2,1,0:T(8,128)(2,1)} fusion(f32[4,4,4,8,128]{4,3,2,1,0:T(8,128)S(1)} %search.1), kind=kLoop, calls=%fused_computation.1 | loop fusion | flops 65536 | bytes 393216 | tf_op jit(solution)/shard_map/broadcast_in_dim | solution.py:326
  (5 shorter events, 0.1 us)
Async XLA Ops:
  0.0 28.6 %copy-start.3 = (bf16[64,128]{1,0:T(8,128)(2,1)S(1)}, bf16[64,128]{1,0:T(8,128)(2,1)}, u32[]{:S(2)}) copy-start(bf16[64,128]{1,0:T(8,128)(2,1)} %constant.19.clone.m_ref) | copy-start | bytes 49156
  1.1 10.3 %collective-permute-start = (bf16[1,49152]{1,0:T(2,128)(2,1)S(1)}, bf16[1,49152]{1,0:T(2,128)(2,1)S(1)}, u32[]{:S(2)}, u32[]{:S(2)}) collective-permute-start(bf16[1,49152]{1,0:T(2,128)(2,1)S(1)} %slice.3), channel_id=1, source_target_pairs={{0,2},{1,3},{4,6},{5,7},{8,10},{9,11},{12,14},{13,15},{16,18},{17,... | collective-permute-start | bytes 294920 | tf_op jit(solution)/shard_map/ppermute | solution.py:26
  11.5 0.9 %copy-start = (bf16[256,256]{1,0:T(8,128)(2,1)S(1)}, bf16[256,256]{1,0:T(8,128)(2,1)}, u32[]{:S(2)}) copy-start(bf16[256,256]{1,0:T(8,128)(2,1)} %constant.17.clone.w2_ref) | copy-start | bytes 393220
  12.4 0.9 %copy-start.1 = (f32[2,128,128]{2,1,0:T(8,128)S(1)}, f32[2,128,128]{2,1,0:T(8,128)}, u32[]{:S(2)}) copy-start(f32[2,128,128]{2,1,0:T(8,128)} %constant.18.clone.tw_ref) | copy-start | bytes 393220
  13.3 0.8 %copy-start.2 = (bf16[256,128]{1,0:T(8,128)(2,1)S(1)}, bf16[256,128]{1,0:T(8,128)(2,1)}, u32[]{:S(2)}) copy-start(bf16[256,128]{1,0:T(8,128)(2,1)} %constant.16.clone.w1_ref) | copy-start | bytes 196612

commit v3 on v2

v3 whole, which is shorter than its diff:
```python
import functools
import math

import jax
import jax.numpy as jnp
import numpy as np
from jax import lax
from jax.experimental import pallas as pl
from jax.experimental.pallas import tpu as pltpu
from jax.sharding import PartitionSpec as P

SIDE = 128
NBLK = 64
FD = 4
TT = 8
MAXT = 3
WMAX = 8
SPB = 8
MESH = pl.DeviceIdType.MESH
F32 = jnp.float32
BF16 = jnp.bfloat16


def tables(channels):
    i = np.arange(SIDE)
    ang = (i[:, None] * i[None, :] % SIDE) * (2.0 * math.pi / SIDE)
    c, s = np.cos(ang), np.sin(ang)
    w1 = np.concatenate([c, s], 0)
    w2 = np.block([[c, -s], [-s, -c]])
    tw = (i[:, None] * i[None, :] % channels) * (2.0 * math.pi / channels)
    twiddle = np.stack([np.cos(tw), np.sin(tw)]).astype(np.float32)
    return jnp.asarray(w1, BF16), jnp.asarray(w2, BF16), jnp.asarray(twiddle)


def fine_rows(groups, width):
    g = np.arange(groups)[:, None]
    i = np.arange(width)[None, :]
    fine = g * FD * (width - 1 - i) // (groups * (width - 1))
    hot = np.stack([fine == step for step in range(FD)])
    hot = hot.reshape(FD, groups, width // SIDE, SIDE).transpose(2, 0, 1, 3)
    return jnp.asarray(hot.reshape(-1, SIDE), BF16)


def search_kernel(
    sizes, x_ref, raw_ref, proto_ref, w1_ref, w2_ref, tw_ref, m_ref, delays_ref, widths_ref, owners_ref, out_ref,
    window, early, history, filt, p_ref, band_ref, bands, inv, tot, tail, send, got,
    hist_send, hist_recv, band_send, band_recv, tail_send, tail_recv, own_send, own_recv,
):
    spectra, spec, groups, slabs, owner_count, axes = sizes
    step = pl.program_id(0)
    scale = 1.0 / (4 * SIDE * SIDE)
    frame_size = SIDE * SIDE
    tm = lax.axis_index("tm")

    def peer(axis, shift):
        place = {name: lax.axis_index(name) for name in axes}
        place[axis] = lax.rem(place[axis] + shift, lax.axis_size(axis))
        return tuple(place[name] for name in axes)

    def history_copy():
        size = history.shape[1]
        return pltpu.make_async_remote_copy(
            src_ref=raw_ref.at[:, pl.ds(spec * frame_size - size, size)],
            dst_ref=history,
            send_sem=hist_send,
            recv_sem=hist_recv,
            device_id=peer("tm", 1),
            device_id_type=MESH,
        )

    def unfold(ref, index):
        line = ref[:, index * frame_size : (index + 1) * frame_size]
        return line.astype(F32).reshape(SIDE, SIDE)

    def pair(win, s, start):
        ys = []
        for k in (s, s + 1):
            acc = win[k * SIDE : (k + 1) * SIDE] * filt[0]
            for tap in range(1, 4):
                acc = acc + win[(k + tap) * SIDE : (k + tap + 1) * SIDE] * filt[tap]
            ys.append(acc.astype(BF16))
        a = jnp.dot(w1_ref[...], jnp.concatenate(ys, 1), preferred_element_type=F32)
        ts = []
        for m in range(2):
            re = a[:SIDE, m * SIDE : (m + 1) * SIDE]
            im = a[SIDE:, m * SIDE : (m + 1) * SIDE]
            t_re = re * tw_ref[0] - im * tw_ref[1]
            t_ni = im * tw_ref[0] + re * tw_ref[1]
            ts.append(jnp.concatenate([t_re.astype(BF16), t_ni.astype(BF16)], 1))
        c = jnp.dot(jnp.concatenate(ts, 0), w2_ref[...], preferred_element_type=F32)
        re, im = c[:, :SIDE], c[:, SIDE:]
        power = (re * re + im * im) * scale
        p_ref[pl.ds(start, 2 * SIDE)] = power
        band_ref[...] += power[:SIDE] + power[SIDE:]

    @pl.when(step == 0)
    def _():
        barrier = pltpu.get_barrier_semaphore()
        for off in range(1, slabs):
            pl.semaphore_signal(barrier, inc=1, device_id=peer("tm", off), device_id_type=MESH)
        for off in range(1, owner_count):
            pl.semaphore_signal(barrier, inc=1, device_id=peer("dm", off), device_id_type=MESH)
        pl.semaphore_wait(barrier, slabs + owner_count - 2)
        if slabs > 1:
            history_copy().start()
        for tap in range(4):
            filt[tap] = unfold(proto_ref.at[tap : tap + 1], 0)
        band_ref[...] = jnp.zeros_like(band_ref)
        tot[...] = jnp.zeros_like(tot)
        for k in range(4):
            early[(k + 3) * SIDE : (k + 4) * SIDE] = unfold(x_ref, k)

    @pl.when(step > 0)
    def _():
        for k in range(4):
            window[(k + 3) * SIDE : (k + 4) * SIDE] = unfold(x_ref, k)
        for s in (0, 2):
            pair(window, s, pl.multiple_of((step * SPB + s) * SIDE, SIDE))

    @pl.when(step == 0)
    def _():
        window[4 * SIDE : 7 * SIDE] = early[4 * SIDE : 7 * SIDE]

    for k in range(4, SPB):
        window[(k + 3) * SIDE : (k + 4) * SIDE] = unfold(x_ref, k)
    for s in range(4, SPB, 2):
        pair(window, s, pl.multiple_of((step * SPB + s) * SIDE, SIDE))
    window[: 3 * SIDE] = window[SPB * SIDE :]

    @pl.when(step == spec // SPB - 1)
    def _():
        if slabs > 1:
            history_copy().wait()
            for k in range(3):
                early[k * SIDE : (k + 1) * SIDE] = jnp.where(tm > 0, unfold(history, k), 0.0)
        else:
            early[: 3 * SIDE] = jnp.zeros((3 * SIDE, SIDE), F32)
        for s in (0, 2):
            pair(early, s, s * SIDE)
        finish(
            sizes, peer, m_ref, delays_ref, widths_ref, owners_ref, out_ref,
            p_ref, band_ref, bands, inv, tot, tail, send, got,
            band_send, band_recv, tail_send, tail_recv, own_send, own_recv,
        )


def finish(
    sizes, peer, m_ref, delays_ref, widths_ref, owners_ref, out_ref,
    p_ref, band_ref, bands, inv, tot, tail, send, got,
    band_send, band_recv, tail_send, tail_recv, own_send, own_recv,
):
    spectra, spec, groups, slabs, owner_count, axes = sizes
    halo = MAXT * TT + WMAX - 1
    slots, trials = out_ref.shape[0], out_ref.shape[2]
    quad = trials * groups
    tm, dm = lax.axis_index("tm"), lax.axis_index("dm")

    copies = []
    for off in range(1, slabs):
        copy = pltpu.make_async_remote_copy(
            src_ref=band_ref,
            dst_ref=bands.at[off - 1],
            send_sem=band_send.at[off - 1],
            recv_sem=band_recv.at[off - 1],
            device_id=peer("tm", off),
            device_id_type=MESH,
        )
        copy.start()
        copies.append(copy)
    iota = lambda shape, dim: lax.broadcasted_iota(jnp.int32, shape, dim)
    spread = (iota((NBLK, SIDE), 1) == 2 * iota((NBLK, SIDE), 0)).astype(BF16)
    late = jnp.dot(delays_ref[...].astype(F32).astype(BF16), spread, preferred_element_type=F32)
    on = iota((quad, SIDE), 1) % 2 == 0
    mask = jnp.concatenate(
        [jnp.where(on & (late == float(v)), 1.0, 0.0) for v in range(MAXT + 1)], 0
    ).astype(BF16)
    wide = max(SIDE, quad)
    lane = iota((groups, wide), 1)
    row = iota((groups, wide), 0)
    owner = jnp.broadcast_to(owners_ref[...], (groups, wide))
    mine = jnp.sum(jnp.where(lane // trials == row, owner, 0), 0, keepdims=True)
    rank = jnp.sum(jnp.where((owner == mine) & (row < lane // trials), 1, 0), 0, keepdims=True)
    place = (mine * slots + rank) * trials + lane[:1] % trials
    place = jnp.where(lane[:1] < quad, place, -1)
    rows_out = owner_count * slots * trials
    pack = jnp.where(iota((rows_out, wide), 0) == place, 1.0, 0.0)
    reach = jnp.broadcast_to(widths_ref[...], (widths_ref.shape[0], SIDE))
    root = 1.0 / jnp.sqrt(reach.astype(F32))
    weights = [jnp.where(reach > lag, root, 0.0) for lag in range(WMAX)]

    band = band_ref[...]
    for off in range(1, slabs):
        copies[off - 1].wait()
        band = band + bands[off - 1]
    inv[...] = 1.0 / (band * (1.0 / spectra) + 1e-06)

    even = lax.broadcasted_iota(jnp.int32, (FD * groups, SIDE), 1) % 2 == 0

    def block(step, carry):
        for s in range(0, SPB, 2):
            flats = []
            for k in (s, s + 1):
                start = pl.multiple_of((step * SPB + k) * SIDE, SIDE)
                ratio = p_ref[pl.ds(start, SIDE)] * inv[...]
                mean = jnp.sum(jnp.sum(ratio, 0, keepdims=True), 1, keepdims=True)
                flats.append((ratio - mean * (1.0 / (SIDE * SIDE))).astype(BF16))
            r = jnp.dot(m_ref[...], jnp.concatenate(flats, 1), preferred_element_type=F32)
            for m in range(2):
                part = r[:, m * SIDE : (m + 1) * SIDE]
                part = jnp.where(even, part[: FD * groups], part[FD * groups :])
                for d in range(FD):
                    tot[step * SPB + s + m + d] += part[d * groups : (d + 1) * groups]
        return carry

    blocks = spec // SPB
    last = -(-(halo + FD - 1) // SPB)
    lax.fori_loop(blocks - last, blocks, block, 0)
    if slabs > 1:
        tail_copy = pltpu.make_async_remote_copy(
            src_ref=tot.at[pl.ds(spec - halo, halo + FD - 1)],
            dst_ref=tail,
            send_sem=tail_send,
            recv_sem=tail_recv,
            device_id=peer("tm", 1),
            device_id_type=MESH,
        )
        tail_copy.start()
        lax.fori_loop(0, blocks - last, block, 0)
        tail_copy.wait()
        before = jnp.where(tm > 0, tail[...], 0.0)
    else:
        lax.fori_loop(0, blocks - last, block, 0)
        before = jnp.zeros(tail.shape, F32)

    rows = spec + halo + 1
    ext = jnp.concatenate(
        [
            jnp.zeros((1, groups, SIDE), F32),
            before[:halo],
            tot[: FD - 1] + before[halo:],
            tot[FD - 1 : spec],
        ],
        0,
    ).reshape(rows * groups, SIDE)
    width = SIDE * SIDE // NBLK
    sub = ((ext + pltpu.roll(ext, SIDE - 1, 1)) * (1.0 / math.sqrt(width))).astype(BF16)
    prod = lax.dot_general(
        sub, mask, (((1,), (1,)), ((), ())), preferred_element_type=F32
    )
    lanes = prod.shape[1]
    prod = prod.reshape(rows, groups, lanes)
    lane = lax.broadcasted_iota(jnp.int32, (groups, lanes), 1)
    row = lax.broadcasted_iota(jnp.int32, (groups, lanes), 0)
    own = (lane // trials) % groups == row
    each = jnp.sum(jnp.where(own[None], prod, 0.0), 1)
    count = spec + TT
    dd = 0.0
    for value in range(MAXT + 1):
        start = (MAXT - value) * TT
        dd = dd + each[start : start + count, value * quad : (value + 1) * quad]
    dd = dd * (1.0 / math.sqrt(NBLK))
    if quad < wide:
        dd = jnp.concatenate([dd, jnp.zeros((count, wide - quad), F32)], 1)
    dd = jnp.concatenate([dd, jnp.zeros((2 * SIDE - count, wide), F32)], 0)
    packed = jnp.dot(
        pack, dd.T, preferred_element_type=F32, precision=lax.Precision.HIGHEST
    )
    send[...] = packed.reshape(send.shape)

    copies = []
    for off in range(1, owner_count):
        copy = pltpu.make_async_remote_copy(
            src_ref=send.at[lax.rem(dm + off, owner_count)],
            dst_ref=got.at[dm],
            send_sem=own_send.at[off - 1],
            recv_sem=own_recv.at[off - 1],
            device_id=peer("dm", off),
            device_id_type=MESH,
        )
        copy.start()
        copies.append(copy)
    got[dm] = send[dm]
    for copy in copies:
        copy.wait()

    for d in range(owner_count):
        part = got[d]
        acc = 0.0
        for lag in range(WMAX):
            moved = pltpu.roll(part, 2 * SIDE - (TT - lag), 1)[:, :SIDE]
            acc = acc + moved[:, None, :] * weights[lag][None]
        for s in range(slots):
            out_ref[s, d] = acc[s * trials : (s + 1) * trials]


def shards(axes, raw, proto, delays, widths, owners):
    taps, channels = proto.shape
    spec = raw.shape[1] // channels
    groups, trials, _ = delays.shape
    slabs, owner_count = lax.axis_size("tm"), lax.axis_size("dm")
    capacity = 2 * (groups // owner_count)
    halo = MAXT * TT + WMAX - 1
    w1, w2, tw = tables(channels)
    masks = fine_rows(groups, channels // NBLK)
    sizes = (spec * slabs, spec, groups, slabs, owner_count, axes)
    block = pltpu.VMEM((owner_count, capacity * trials, 2 * SIDE), F32)
    sems = lambda n: pltpu.SemaphoreType.DMA((max(n, 1),))
    full = lambda shape: pl.BlockSpec(shape, lambda i: (0,) * len(shape))
    small = [proto, w1, w2, tw, masks, delays.reshape(groups * trials, NBLK), widths[:, None], owners]
    out = (capacity, owner_count, trials, widths.shape[0], spec)
    box = pl.pallas_call(
        functools.partial(search_kernel, sizes),
        grid=(spec // SPB,),
        in_specs=[
            pl.BlockSpec((1, SPB * channels), lambda i: (0, i)),
            pl.BlockSpec(memory_space=pl.ANY),
            *[full(value.shape) for value in small],
        ],
        out_specs=full(out),
        out_shape=jax.ShapeDtypeStruct(out, F32),
        scratch_shapes=[
            pltpu.VMEM(((SPB + 3) * SIDE, SIDE), F32),
            pltpu.VMEM((7 * SIDE, SIDE), F32),
            pltpu.VMEM((1, 3 * channels), BF16),
            pltpu.VMEM((taps, SIDE, SIDE), F32),
            pltpu.VMEM((spec * SIDE, SIDE), F32),
            pltpu.VMEM((SIDE, SIDE), F32),
            pltpu.VMEM((max(slabs - 1, 1), SIDE, SIDE), F32),
            pltpu.VMEM((SIDE, SIDE), F32),
            pltpu.VMEM((spec + FD - 1, groups, SIDE), F32),
            pltpu.VMEM((halo + FD - 1, groups, SIDE), F32),
            block,
            block,
            pltpu.SemaphoreType.DMA,
            pltpu.SemaphoreType.DMA,
            sems(slabs - 1),
            sems(slabs - 1),
            pltpu.SemaphoreType.DMA,
            pltpu.SemaphoreType.DMA,
            sems(owner_count - 1),
            sems(owner_count - 1),
        ],
        compiler_params=pltpu.CompilerParams(
            vmem_limit_bytes=56 << 20, collective_id=0, has_side_effects=True
        ),
        name="search",
    )(raw, raw, *small)
    return box.astype(BF16)[:, :, None]


def solution(mesh):
    return jax.shard_map(
        functools.partial(shards, mesh.axis_names),
        mesh=mesh,
        in_specs=(P(("group", "dm", "beam"), "tm"), P(), P(), P(), P()),
        out_specs=P("dm", "group", "beam", None, None, "tm"),
        check_vma=False,
    )
```

time: 46.7 us -> 41.6 us (0.89)
  Pallas kernels: 31.2 us -> 36.8 us
  starting transfers between devices: 4.85 us -> 0 us
  local copies, waits for them, and re-layouts: 6.07 us -> 2.64 us
  other arithmetic: 3.86 us -> 1.62 us
    pallas_call x2 -> x1, Pallas kernels: 31.2 us -> 36.8 us  [shards(): pl.pallas_call(functools.partial(search_kernel, sizes), grid=(spec // SPB...]
    ppermute x1 -> x0, starting transfers between devices: 4.85 us -> none  [shifted(): lax.ppermute(value, axis, [(s, s + steps) for s in range(count - steps)])]
    unnamed x9 -> x1, local copies, waits for them, and re-layouts: 3.62 us -> 1.32 us
    broadcast_in_dim x1, local copies, waits for them, and re-layouts: 0.07 us -> 1.32 us  [shards(): widths[:, None]]
    slice x1 -> x0, local copies, waits for them, and re-layouts: 1.14 us -> none  [shards(): before = shifted(raw[:, raw.shape[1] - (taps - 1) * channels:], 'tm', 1)]
    broadcast_in_dim x1, other arithmetic: 0.67 us -> 1.62 us  [shards(): return box.astype(BF16)[:, :, None]]
    reduce_sum x1 -> x0, other arithmetic: 0.91 us -> none  [slot_table(): jnp.sum((same & (index[None, :] < index[:, None])).astype(jnp.int32), 1)]
    eq x3 -> x0, local copies, waits for them, and re-layouts: 0.83 us -> none  [shards(): hit = (delays[None] == value).reshape(-1, NBLK).T]
  transfers between devices with their start and end apart: 1 -> 0, of which waited for: 0 -> 0; matrix products, arithmetic and copies ran while one was open for 12% -> 0% of each run, Pallas kernels for 0% -> 0%
where the time goes in v3:
time: 41.6 us; the launch traced here: 41.1 us
  Pallas kernels  36.8 us (88%)
  local copies, waits for them, and re-layouts  2.64 us (6%)
  other arithmetic  1.62 us (4%)
    pallas_call x1, Pallas kernels, shards(): pl.pallas_call(functools.partial(search_kernel, sizes), grid=(spec // SPB...  36.8 us
    broadcast_in_dim x1, other arithmetic, shards(): return box.astype(BF16)[:, :, None]  1.62 us
    broadcast_in_dim x1, local copies, waits for them, and re-layouts, shards(): widths[:, None]  1.32 us
    unnamed x1, local copies, waits for them, and re-layouts  1.32 us

profile of v3, /device:TPU:0, one launch (start us, length us, event | category | flops | bytes accessed | tf_op | source)
XLA Modules:
  0.0 41.1 jit_solution(8348734993918130488)
XLA Ops:
  0.0 1.3 %copy.10.widths_ref = s32[8,1]{1,0:T(8,128)} copy(s32[8,1]{0,1:T(1,128)} %bitcast.7) | data formatting | bytes 64 | tf_op jit(solution)/shard_map/broadcast_in_dim | solution.py:309
  1.3 1.3 %copy.11.owners_ref = s32[8,1]{1,0:T(8,128)} copy(s32[8,1]{0,1:T(1,128)} %param.13) | data formatting | bytes 64 | tf_op args[4]
  2.6 36.8 %search.1 = f32[4,4,4,8,128]{4,3,2,1,0:T(8,128)} custom-call(bf16[1,2097152]{1,0:T(2,128)(2,1)} %raw_ref.1, bf16[1,2097152]{1,0:T(2,128)(2,1)} %raw_ref.1, f32[4,16384]{1,0:T(4,128)} %proto_ref.1, bf16[256,128]{1,0:T(8,128)(2,1)} %constant.8.clone.w1_ref, bf16[256,256]{1,0:T(8,128)(2,1)} %constant.9.clone.w2_ref, f32[2,128,128]{2,1,0:T(8,128)} %constant.10.clone.tw_ref, ...), custom_call_target="tpu_custom_call" | custom-call | tf_op jit(solution)/shard_map/search/pallas_call | solution.py:311
  39.5 1.6 %convert_bitcast_fusion = bf16[4,4,1,4,8,128]{5,4,3,2,1,0:T(8,128)(2,1)} fusion(f32[4,4,4,8,128]{4,3,2,1,0:T(8,128)} %search.1), kind=kLoop, calls=%fused_computation | loop fusion | flops 65536 | bytes 393216 | tf_op jit(solution)/shard_map/broadcast_in_dim | solution.py:348

commit v4 on v3

--- a/solution.py
+++ b/solution.py
@@ -16,6 +16,8 @@
 MAXT = 3
 WMAX = 8
 SPB = 8
+HALF = SIDE // 2
+FR = 80
 MESH = pl.DeviceIdType.MESH
 F32 = jnp.float32
 BF16 = jnp.bfloat16
@@ -25,10 +27,10 @@
     i = np.arange(SIDE)
     ang = (i[:, None] * i[None, :] % SIDE) * (2.0 * math.pi / SIDE)
     c, s = np.cos(ang), np.sin(ang)
-    w1 = np.concatenate([c, s], 0)
+    w1 = np.concatenate([c[:FR], s[:FR]], 0)
     w2 = np.block([[c, -s], [-s, -c]])
     tw = (i[:, None] * i[None, :] % channels) * (2.0 * math.pi / channels)
-    twiddle = np.stack([np.cos(tw), np.sin(tw)]).astype(np.float32)
+    twiddle = np.stack([np.cos(tw[:FR]), np.sin(tw[:FR])]).astype(np.float32)
     return jnp.asarray(w1, BF16), jnp.asarray(w2, BF16), jnp.asarray(twiddle)
 
 
@@ -38,12 +40,15 @@
     fine = g * FD * (width - 1 - i) // (groups * (width - 1))
     hot = np.stack([fine == step for step in range(FD)])
     hot = hot.reshape(FD, groups, width // SIDE, SIDE).transpose(2, 0, 1, 3)
-    return jnp.asarray(hot.reshape(-1, SIDE), BF16)
+    out = np.zeros((2, 2, FD, groups, FR))
+    out[0, ..., : HALF + 1] = hot[..., : HALF + 1]
+    out[1, ..., 1:HALF] = hot[..., : HALF : -1]
+    return jnp.asarray(out.reshape(-1, FR), BF16)
 
 
 def search_kernel(
     sizes, x_ref, raw_ref, proto_ref, w1_ref, w2_ref, tw_ref, m_ref, delays_ref, widths_ref, owners_ref, out_ref,
-    window, early, history, filt, p_ref, band_ref, bands, inv, tot, tail, send, got,
+    window, early, history, filt, p_ref, band_ref, bands, inv, direct, mirror, tot, tail, send, got,
     hist_send, hist_recv, band_send, band_recv, tail_send, tail_recv, own_send, own_recv,
 ):
     spectra, spec, groups, slabs, owner_count, axes = sizes
@@ -82,16 +87,16 @@
         a = jnp.dot(w1_ref[...], jnp.concatenate(ys, 1), preferred_element_type=F32)
         ts = []
         for m in range(2):
-            re = a[:SIDE, m * SIDE : (m + 1) * SIDE]
-            im = a[SIDE:, m * SIDE : (m + 1) * SIDE]
+            re = a[:FR, m * SIDE : (m + 1) * SIDE]
+            im = a[FR:, m * SIDE : (m + 1) * SIDE]
             t_re = re * tw_ref[0] - im * tw_ref[1]
             t_ni = im * tw_ref[0] + re * tw_ref[1]
             ts.append(jnp.concatenate([t_re.astype(BF16), t_ni.astype(BF16)], 1))
         c = jnp.dot(jnp.concatenate(ts, 0), w2_ref[...], preferred_element_type=F32)
         re, im = c[:, :SIDE], c[:, SIDE:]
         power = (re * re + im * im) * scale
-        p_ref[pl.ds(start, 2 * SIDE)] = power
-        band_ref[...] += power[:SIDE] + power[SIDE:]
+        p_ref[pl.ds(start, 2 * FR)] = power
+        band_ref[...] += power[:FR] + power[FR:]
 
     @pl.when(step == 0)
     def _():
@@ -106,7 +111,8 @@
         for tap in range(4):
             filt[tap] = unfold(proto_ref.at[tap : tap + 1], 0)
         band_ref[...] = jnp.zeros_like(band_ref)
-        tot[...] = jnp.zeros_like(tot)
+        direct[...] = jnp.zeros_like(direct)
+        mirror[...] = jnp.zeros_like(mirror)
         for k in range(4):
             early[(k + 3) * SIDE : (k + 4) * SIDE] = unfold(x_ref, k)
 
@@ -115,7 +121,7 @@
         for k in range(4):
             window[(k + 3) * SIDE : (k + 4) * SIDE] = unfold(x_ref, k)
         for s in (0, 2):
-            pair(window, s, pl.multiple_of((step * SPB + s) * SIDE, SIDE))
+            pair(window, s, pl.multiple_of((step * SPB + s) * FR, FR))
 
     @pl.when(step == 0)
     def _():
@@ -124,7 +130,7 @@
     for k in range(4, SPB):
         window[(k + 3) * SIDE : (k + 4) * SIDE] = unfold(x_ref, k)
     for s in range(4, SPB, 2):
-        pair(window, s, pl.multiple_of((step * SPB + s) * SIDE, SIDE))
+        pair(window, s, pl.multiple_of((step * SPB + s) * FR, FR))
     window[: 3 * SIDE] = window[SPB * SIDE :]
 
     @pl.when(step == spec // SPB - 1)
@@ -136,17 +142,17 @@
         else:
             early[: 3 * SIDE] = jnp.zeros((3 * SIDE, SIDE), F32)
         for s in (0, 2):
-            pair(early, s, s * SIDE)
+            pair(early, s, s * FR)
         finish(
             sizes, peer, m_ref, delays_ref, widths_ref, owners_ref, out_ref,
-            p_ref, band_ref, bands, inv, tot, tail, send, got,
+            p_ref, band_ref, bands, inv, direct, mirror, tot, tail, send, got,
             band_send, band_recv, tail_send, tail_recv, own_send, own_recv,
         )
 
 
 def finish(
     sizes, peer, m_ref, delays_ref, widths_ref, owners_ref, out_ref,
-    p_ref, band_ref, bands, inv, tot, tail, send, got,
+    p_ref, band_ref, bands, inv, direct, mirror, tot, tail, send, got,
     band_send, band_recv, tail_send, tail_recv, own_send, own_recv,
 ):
     spectra, spec, groups, slabs, owner_count, axes = sizes
@@ -174,17 +180,22 @@
     mask = jnp.concatenate(
         [jnp.where(on & (late == float(v)), 1.0, 0.0) for v in range(MAXT + 1)], 0
     ).astype(BF16)
+    def column(ref):
+        n = ref.shape[1]
+        same = iota((n, n), 0) == iota((n, n), 1)
+        return jnp.sum(jnp.where(same, jnp.broadcast_to(ref[...], (n, n)), 0), 1, keepdims=True)
+
     wide = max(SIDE, quad)
     lane = iota((groups, wide), 1)
     row = iota((groups, wide), 0)
-    owner = jnp.broadcast_to(owners_ref[...], (groups, wide))
+    owner = jnp.broadcast_to(column(owners_ref), (groups, wide))
     mine = jnp.sum(jnp.where(lane // trials == row, owner, 0), 0, keepdims=True)
     rank = jnp.sum(jnp.where((owner == mine) & (row < lane // trials), 1, 0), 0, keepdims=True)
     place = (mine * slots + rank) * trials + lane[:1] % trials
     place = jnp.where(lane[:1] < quad, place, -1)
     rows_out = owner_count * slots * trials
     pack = jnp.where(iota((rows_out, wide), 0) == place, 1.0, 0.0)
-    reach = jnp.broadcast_to(widths_ref[...], (widths_ref.shape[0], SIDE))
+    reach = jnp.broadcast_to(column(widths_ref), (widths_ref.shape[1], SIDE))
     root = 1.0 / jnp.sqrt(reach.astype(F32))
     weights = [jnp.where(reach > lag, root, 0.0) for lag in range(WMAX)]
 
@@ -192,7 +203,8 @@
     for off in range(1, slabs):
         copies[off - 1].wait()
         band = band + bands[off - 1]
-    inv[...] = 1.0 / (band * (1.0 / spectra) + 1e-06)
+    held = lax.broadcasted_iota(jnp.int32, (FR, SIDE), 0) <= HALF
+    inv[...] = jnp.where(held, 1.0 / (band * (1.0 / spectra) + 1e-06), 0.0)
 
     even = lax.broadcasted_iota(jnp.int32, (FD * groups, SIDE), 1) % 2 == 0
 
@@ -200,21 +212,39 @@
         for s in range(0, SPB, 2):
             flats = []
             for k in (s, s + 1):
-                start = pl.multiple_of((step * SPB + k) * SIDE, SIDE)
-                ratio = p_ref[pl.ds(start, SIDE)] * inv[...]
-                mean = jnp.sum(jnp.sum(ratio, 0, keepdims=True), 1, keepdims=True)
-                flats.append((ratio - mean * (1.0 / (SIDE * SIDE))).astype(BF16))
+                start = pl.multiple_of((step * SPB + k) * FR, FR)
+                ratio = p_ref[pl.ds(start, FR)] * inv[...]
+                line = 2.0 * jnp.sum(ratio, 0, keepdims=True) - ratio[:1] - ratio[HALF : HALF + 1]
+                mean = jnp.sum(line, 1, keepdims=True) * (1.0 / (SIDE * SIDE))
+                flats.append((ratio - mean).astype(BF16))
             r = jnp.dot(m_ref[...], jnp.concatenate(flats, 1), preferred_element_type=F32)
+            size = FD * groups
             for m in range(2):
                 part = r[:, m * SIDE : (m + 1) * SIDE]
-                part = jnp.where(even, part[: FD * groups], part[FD * groups :])
+                one = jnp.where(even, part[:size], part[size : 2 * size])
+                two = jnp.where(even, part[3 * size :], part[2 * size : 3 * size])
                 for d in range(FD):
-                    tot[step * SPB + s + m + d] += part[d * groups : (d + 1) * groups]
+                    direct[step * SPB + s + m + d] += one[d * groups : (d + 1) * groups]
+                    mirror[step * SPB + s + m + d] += two[d * groups : (d + 1) * groups]
         return carry
 
+    def combine(first, stop):
+        one = direct[first:stop].reshape(-1, SIDE)
+        two = mirror[first:stop].reshape(-1, SIDE)
+        high = two.astype(BF16)
+        low = (two - high.astype(F32)).astype(BF16)
+        both = jnp.concatenate([high, low], 1)
+        turned = jnp.dot(both, turn, preferred_element_type=F32)
+        total = one + pltpu.roll(one, SIDE - 1, 1) + turned
+        tot[first:stop] = total.reshape(stop - first, groups, SIDE)
+
+    source = iota((2 * SIDE, SIDE), 0) % SIDE
+    goal = iota((2 * SIDE, SIDE), 1)
+    turn = jnp.where((goal % 2 == 0) & (source // 2 == HALF - 1 - goal // 2), 1.0, 0.0).astype(BF16)
     blocks = spec // SPB
     last = -(-(halo + FD - 1) // SPB)
     lax.fori_loop(blocks - last, blocks, block, 0)
+    combine(spec - halo, spec + FD - 1)
     if slabs > 1:
         tail_copy = pltpu.make_async_remote_copy(
             src_ref=tot.at[pl.ds(spec - halo, halo + FD - 1)],
@@ -226,10 +256,12 @@
         )
         tail_copy.start()
         lax.fori_loop(0, blocks - last, block, 0)
+        combine(0, spec - halo)
         tail_copy.wait()
         before = jnp.where(tm > 0, tail[...], 0.0)
     else:
         lax.fori_loop(0, blocks - last, block, 0)
+        combine(0, spec - halo)
         before = jnp.zeros(tail.shape, F32)
 
     rows = spec + halo + 1
@@ -243,7 +275,7 @@
         0,
     ).reshape(rows * groups, SIDE)
     width = SIDE * SIDE // NBLK
-    sub = ((ext + pltpu.roll(ext, SIDE - 1, 1)) * (1.0 / math.sqrt(width))).astype(BF16)
+    sub = (ext * (1.0 / math.sqrt(width))).astype(BF16)
     prod = lax.dot_general(
         sub, mask, (((1,), (1,)), ((), ())), preferred_element_type=F32
     )
@@ -306,7 +338,7 @@
     block = pltpu.VMEM((owner_count, capacity * trials, 2 * SIDE), F32)
     sems = lambda n: pltpu.SemaphoreType.DMA((max(n, 1),))
     full = lambda shape: pl.BlockSpec(shape, lambda i: (0,) * len(shape))
-    small = [proto, w1, w2, tw, masks, delays.reshape(groups * trials, NBLK), widths[:, None], owners]
+    small = [proto, w1, w2, tw, masks, delays.reshape(groups * trials, NBLK), widths[None], owners.T]
     out = (capacity, owner_count, trials, widths.shape[0], spec)
     box = pl.pallas_call(
         functools.partial(search_kernel, sizes),
@@ -323,10 +355,12 @@
             pltpu.VMEM((7 * SIDE, SIDE), F32),
             pltpu.VMEM((1, 3 * channels), BF16),
             pltpu.VMEM((taps, SIDE, SIDE), F32),
-            pltpu.VMEM((spec * SIDE, SIDE), F32),
-            pltpu.VMEM((SIDE, SIDE), F32),
-            pltpu.VMEM((max(slabs - 1, 1), SIDE, SIDE), F32),
-            pltpu.VMEM((SIDE, SIDE), F32),
+            pltpu.VMEM((spec * FR, SIDE), F32),
+            pltpu.VMEM((FR, SIDE), F32),
+            pltpu.VMEM((max(slabs - 1, 1), FR, SIDE), F32),
+            pltpu.VMEM((FR, SIDE), F32),
+            pltpu.VMEM((spec + FD - 1, groups, SIDE), F32),
+            pltpu.VMEM((spec + FD - 1, groups, SIDE), F32),
             pltpu.VMEM((spec + FD - 1, groups, SIDE), F32),
             pltpu.VMEM((halo + FD - 1, groups, SIDE), F32),
             block,

time: 41.6 us -> 38 us (0.913)
  local copies, waits for them, and re-layouts: 2.64 us -> 0 us
  Pallas kernels: 36.8 us -> 36 us
    broadcast_in_dim x1 -> x0, local copies, waits for them, and re-layouts: 1.32 us -> none  [shards(): widths[:, None]]
    unnamed x1 -> x0, local copies, waits for them, and re-layouts: 1.32 us -> none
    pallas_call x1, Pallas kernels: 36.8 us -> 36 us  [shards(): pl.pallas_call(functools.partial(search_kernel, sizes), grid=(spec // SPB...]
where the time goes in v4:
time: 38 us; the launch traced here: 37.6 us
  Pallas kernels  36 us (95%)
  other arithmetic  1.62 us (4%)
    pallas_call x1, Pallas kernels, shards(): pl.pallas_call(functools.partial(search_kernel, sizes), grid=(spec // SPB...  36 us
    broadcast_in_dim x1, other arithmetic, shards(): return box.astype(BF16)[:, :, None]  1.62 us

profile of v4, /device:TPU:0, one launch (start us, length us, event | category | flops | bytes accessed | tf_op | source)
XLA Modules:
  0.0 37.6 jit_solution(3830762504397453773)
XLA Ops:
  0.0 36.0 %search.1 = f32[4,4,4,8,128]{4,3,2,1,0:T(8,128)} custom-call(bf16[1,2097152]{1,0:T(2,128)(2,1)} %raw_ref.1, bf16[1,2097152]{1,0:T(2,128)(2,1)} %raw_ref.1, f32[4,16384]{1,0:T(4,128)} %proto_ref.1, bf16[160,128]{1,0:T(8,128)(2,1)} %constant.8.clone.w1_ref, bf16[256,256]{1,0:T(8,128)(2,1)} %constant.9.clone.w2_ref, f32[2,80,128]{2,1,0:T(8,128)} %constant.10.clone.tw_ref, ...), custom_call_target="tpu_custom_call" | custom-call | tf_op jit(solution)/shard_map/search/pallas_call | solution.py:343
  36.0 1.6 %convert_bitcast_fusion = bf16[4,4,1,4,8,128]{5,4,3,2,1,0:T(8,128)(2,1)} fusion(f32[4,4,4,8,128]{4,3,2,1,0:T(8,128)} %search.1), kind=kLoop, calls=%fused_computation | loop fusion | flops 65536 | bytes 393216 | tf_op jit(solution)/shard_map/broadcast_in_dim | solution.py:382

commit v5 on v4

--- a/solution.py
+++ b/solution.py
@@ -15,7 +15,7 @@
 TT = 8
 MAXT = 3
 WMAX = 8
-SPB = 8
+SPB = 32
 HALF = SIDE // 2
 FR = 80
 MESH = pl.DeviceIdType.MESH
@@ -157,7 +157,8 @@
 ):
     spectra, spec, groups, slabs, owner_count, axes = sizes
     halo = MAXT * TT + WMAX - 1
-    slots, trials = out_ref.shape[0], out_ref.shape[2]
+    slots = out_ref.shape[0]
+    trials = out_ref.shape[2] // widths_ref.shape[1]
     quad = trials * groups
     tm, dm = lax.axis_index("tm"), lax.axis_index("dm")
 
@@ -322,7 +323,8 @@
             moved = pltpu.roll(part, 2 * SIDE - (TT - lag), 1)[:, :SIDE]
             acc = acc + moved[:, None, :] * weights[lag][None]
         for s in range(slots):
-            out_ref[s, d] = acc[s * trials : (s + 1) * trials]
+            part = acc[s * trials : (s + 1) * trials].reshape(-1, SIDE)
+            out_ref[s, d] = part.astype(BF16)
 
 
 def shards(axes, raw, proto, delays, widths, owners):
@@ -339,7 +341,7 @@
     sems = lambda n: pltpu.SemaphoreType.DMA((max(n, 1),))
     full = lambda shape: pl.BlockSpec(shape, lambda i: (0,) * len(shape))
     small = [proto, w1, w2, tw, masks, delays.reshape(groups * trials, NBLK), widths[None], owners.T]
-    out = (capacity, owner_count, trials, widths.shape[0], spec)
+    out = (capacity, owner_count, trials * widths.shape[0], spec)
     box = pl.pallas_call(
         functools.partial(search_kernel, sizes),
         grid=(spec // SPB,),
@@ -349,7 +351,7 @@
             *[full(value.shape) for value in small],
         ],
         out_specs=full(out),
-        out_shape=jax.ShapeDtypeStruct(out, F32),
+        out_shape=jax.ShapeDtypeStruct(out, BF16),
         scratch_shapes=[
             pltpu.VMEM(((SPB + 3) * SIDE, SIDE), F32),
             pltpu.VMEM((7 * SIDE, SIDE), F32),
@@ -379,7 +381,7 @@
         ),
         name="search",
     )(raw, raw, *small)
-    return box.astype(BF16)[:, :, None]
+    return box.reshape(capacity, owner_count, 1, trials, widths.shape[0], spec)
 
 
 def solution(mesh):

time: 38 us -> 29.9 us (0.79)
  Pallas kernels: 36 us -> 28.2 us
  other arithmetic: 1.62 us -> 0 us
  local copies, waits for them, and re-layouts: 0 us -> 1.57 us
    pallas_call x1, Pallas kernels: 36 us -> 28.2 us  [shards(): pl.pallas_call(functools.partial(search_kernel, sizes), grid=(spec // SPB...]
    broadcast_in_dim x1 -> x0, other arithmetic: 1.62 us -> none  [shards(): return box.astype(BF16)[:, :, None]]
    unnamed x0 -> x1, local copies, waits for them, and re-layouts: none -> 1.57 us
where the time goes in v5:
time: 29.9 us; the launch traced here: 29.8 us
  Pallas kernels  28.2 us (94%)
  local copies, waits for them, and re-layouts  1.57 us (5%)
    pallas_call x1, Pallas kernels, shards(): pl.pallas_call(functools.partial(search_kernel, sizes), grid=(spec // SPB...  28.2 us
    unnamed x1, local copies, waits for them, and re-layouts  1.57 us

profile of v5, /device:TPU:0, one launch (start us, length us, event | category | flops | bytes accessed | tf_op | source)
XLA Modules:
  0.0 29.8 jit_solution(11133890146073481167)
XLA Ops:
  0.0 28.2 %search.1 = bf16[4,4,32,128]{3,2,1,0:T(8,128)(2,1)} custom-call(bf16[1,2097152]{1,0:T(2,128)(2,1)} %raw_ref.1, bf16[1,2097152]{1,0:T(2,128)(2,1)} %raw_ref.1, f32[4,16384]{1,0:T(4,128)} %proto_ref.1, bf16[160,128]{1,0:T(8,128)(2,1)} %constant.8.clone.w1_ref, bf16[256,256]{1,0:T(8,128)(2,1)} %constant.9.clone.w2_ref, f32[2,80,128]{2,1,0:T(8,128)} %constant.10.clone.tw_ref, ...), custom_call_target="tpu_custom_call" | custom-call | tf_op jit(solution)/shard_map/search/pallas_call | solution.py:345
  28.2 1.6 %copy.12 = bf16[4,4,1,4,8,128]{5,4,3,2,1,0:T(8,128)(2,1)} copy(bf16[4,4,1,4,8,128]{5,4,3,2,1,0:T(8,128)(2,1)} %bitcast.6) | data formatting | bytes 262144
